TPU v7x, 256 devices: a whole 4x4x8 slice. The times are simulated.
256 devices in a mesh: dp: 16 (over y_lo, z), seq: 16 (over x, y_hi, core).
Axes of the slice: x: 4, y: 4 (y_hi: 2, y_lo: 2; y = y_hi * 2 + y_lo), z: 8, core: 2. Of those that a mesh axis runs over, the one named last changes fastest.
Arguments:
- seq_embed: bfloat16 [16, 3072, 1536], P('dp', 'seq'), may hold values from -24 to 24
- w_qkv: bfloat16 [1536, 2304], P('seq'), may hold values from -1 to 1
- upstream: bfloat16 [16, 3072, 768], P('dp', 'seq'), may hold values from -6 to 6
Outputs:
- attended: bfloat16 [16, 3072, 768], P('dp', 'seq')
- grad_input: bfloat16 [16, 3072, 1536], P('dp', 'seq')
- grad_qkv: bfloat16 [1536, 2304], P('seq')
All inputs are finite; a program needn't handle non-finite values.
Results may differ from a plain program's by a relative error of at most 0.04.
Values may be sent and summed in bfloat16 or wider, within the bound.
A program may use at most 128 MiB of HBM per device.

v0:
```python
import math

import jax
import jax.numpy as jnp
from jax import lax
from jax.sharding import PartitionSpec as P

HEADS = 6


def split_heads(block, heads):
    return block.reshape(block.shape[0], heads, block.shape[1] // heads)


def on_device(seq_embed, w_qkv, upstream):
    heads = HEADS
    width = upstream.shape[-1]
    head_dim = width // heads
    score_scale = 1.0 / math.sqrt(head_dim)
    weights = lax.all_gather(w_qkv, "seq", axis=0, tiled=True)
    tokens = seq_embed[0]
    grad_out = upstream[0]
    rows_here = tokens.shape[0]
    projected = jnp.dot(tokens, weights, preferred_element_type=jnp.float32).astype(jnp.bfloat16)
    queries = projected[:, :width]
    keys_here = projected[:, width : 2 * width]
    values_here = projected[:, 2 * width :]
    keys_all, values_all = (
        lax.all_gather(keys_here, "seq", axis=0, tiled=True),
        lax.all_gather(values_here, "seq", axis=0, tiled=True),
    )
    query_heads = split_heads(queries, heads)
    key_heads = split_heads(keys_all, heads)
    value_heads = split_heads(values_all, heads)
    scores = (
        jnp.einsum("qhd,khd->hqk", query_heads, key_heads, preferred_element_type=jnp.float32)
        * score_scale
    )
    peak = jnp.max(scores, axis=-1, keepdims=True)
    log_total = peak[..., 0] + jnp.log(jnp.sum(jnp.exp(scores - peak), axis=-1))
    probs = jnp.exp(scores - log_total[..., None])
    probs_low = probs.astype(jnp.bfloat16)
    attended_heads = jnp.einsum(
        "hqk,khd->qhd", probs_low, value_heads, preferred_element_type=jnp.float32
    ).astype(jnp.bfloat16)
    grad_heads = split_heads(grad_out, heads)
    delta_rows = jnp.sum(
        grad_heads.astype(jnp.float32) * attended_heads.astype(jnp.float32), axis=-1
    )
    grad_probs = jnp.einsum(
        "qhd,khd->hqk", grad_heads, value_heads, preferred_element_type=jnp.float32
    )
    grad_scores = (probs * (grad_probs - delta_rows.T[..., None]) * score_scale).astype(
        jnp.bfloat16
    )
    grad_queries = jnp.einsum(
        "hqk,khd->qhd", grad_scores, key_heads, preferred_element_type=jnp.float32
    ).astype(jnp.bfloat16)
    lse_all, delta_all = (
        lax.all_gather(log_total.T, "seq", axis=0, tiled=True),
        lax.all_gather(delta_rows, "seq", axis=0, tiled=True),
    )
    key_local = split_heads(keys_here, heads)
    value_local = split_heads(values_here, heads)
    query_piece = split_heads(lax.all_gather(queries, "seq", axis=0, tiled=True), heads)
    grad_piece = split_heads(lax.all_gather(grad_out, "seq", axis=0, tiled=True), heads)
    lse_piece = lse_all.T
    delta_piece = delta_all.T
    piece_scores = (
        jnp.einsum("qhd,khd->hqk", query_piece, key_local, preferred_element_type=jnp.float32)
        * score_scale
    )
    piece_probs = jnp.exp(piece_scores - lse_piece[..., None])
    grad_values = jnp.einsum(
        "hqk,qhd->khd",
        piece_probs.astype(jnp.bfloat16),
        grad_piece,
        preferred_element_type=jnp.float32,
    )
    piece_grad_probs = jnp.einsum(
        "qhd,khd->hqk", grad_piece, value_local, preferred_element_type=jnp.float32
    )
    piece_grad_scores = (
        piece_probs * (piece_grad_probs - delta_piece[..., None]) * score_scale
    ).astype(jnp.bfloat16)
    grad_keys = jnp.einsum(
        "hqk,qhd->khd", piece_grad_scores, query_piece, preferred_element_type=jnp.float32
    )
    grad_keys, grad_values = (grad_keys, grad_values)
    grad_proj = jnp.concatenate(
        [
            grad_queries.reshape(rows_here, width),
            grad_keys.astype(jnp.bfloat16).reshape(rows_here, width),
            grad_values.astype(jnp.bfloat16).reshape(rows_here, width),
        ],
        axis=1,
    )
    grad_input = lax.dot_general(
        grad_proj, weights, (((1,), (1,)), ((), ())), preferred_element_type=jnp.float32
    ).astype(jnp.bfloat16)
    term = lax.dot_general(
        tokens, grad_proj, (((0,), (0,)), ((), ())), preferred_element_type=jnp.float32
    )
    summed = lax.psum_scatter(
        lax.optimization_barrier(term.astype(jnp.bfloat16))
        .astype(jnp.float32)
        .astype(jnp.bfloat16),
        "seq",
        scatter_dimension=0,
        tiled=True,
    )
    total = lax.psum(summed, "dp").astype(jnp.float32)
    attended = attended_heads.reshape(rows_here, width)
    return (attended[None], grad_input[None], total.astype(jnp.bfloat16))


def solution(mesh):
    placed = (P("dp", "seq", None), P("seq", None), P("dp", "seq", None))
    return jax.shard_map(
        on_device,
        mesh=mesh,
        in_specs=placed,
        out_specs=(P("dp", "seq", None), P("dp", "seq", None), P("seq", None)),
        check_vma=False,
    )
```

profile of v0, /device:TPU:2, one launch (start us, length us, event | category | flops | bytes accessed | tf_op | source)
XLA Modules:
  0.0 663.6 jit_solution(6117910122317396261)
XLA Ops:
  8.7 76.5 %all-gather.9.cloned.1.call-done = bf16[1536,2304]{1,0:T(8,128)(2,1)} async-done(((bf16[96,2304]{1,0:T(8,128)(2,1)}), bf16[1536,2304]{1,0:T(8,128)(2,1)}) %all-gather.9.cloned.1.call-update) | async-done | bytes 7077904 | tf_op jit(solution)/shard_map/all_gather | solution.py:20
  85.2 4.5 convolution_convert_fusion.1
  92.3 57.5 %all-gather.17.cloned.1.call-done = bf16[1,3072,768]{2,1,0:T(8,128)(2,1)} async-done(((bf16[1,192,768]{2,1,0:T(8,128)(2,1)}), bf16[1,3072,768]{2,1,0:T(8,128)(2,1)}) %all-gather.17.cloned.1.call-update) | async-done | bytes 4718608 | tf_op jit(solution)/shard_map/all_gather | solution.py:66
  149.8 6.7 %copy.47 = bf16[1,3072,768]{1,2,0:T(8,128)(2,1)} copy(bf16[1,3072,768]{2,1,0:T(8,128)(2,1)} %all-gather.17.cloned.1.call-done) | data formatting | bytes 9437184 | tf_op jit(solution)/shard_map/all_gather | solution.py:66
  156.5 58.5 %all-gather.11.cloned.1.call-done = bf16[3072,768]{1,0:T(8,128)(2,1)} async-done(((bf16[192,768]{1,0:T(8,128)(2,1)}), bf16[3072,768]{1,0:T(8,128)(2,1)}) %all-gather.11.cloned.1.call-update) | async-done | bytes 4718608 | tf_op jit(solution)/shard_map/all_gather | solution.py:30
  215.0 6.7 %copy.32 = bf16[3072,768]{0,1:T(8,128)(2,1)} copy(bf16[3072,768]{1,0:T(8,128)(2,1)} %all-gather.11.cloned.1.call-done) | data formatting | bytes 9437184 | tf_op jit(solution)/shard_map/all_gather | solution.py:30
  221.7 58.3 %all-gather.13.cloned.1.call-done = bf16[3072,768]{1,0:T(8,128)(2,1)} async-done(((bf16[192,768]{1,0:T(8,128)(2,1)}), bf16[3072,768]{1,0:T(8,128)(2,1)}) %all-gather.13.cloned.1.call-update) | async-done | bytes 4718608 | tf_op jit(solution)/shard_map/all_gather | solution.py:29
  280.0 6.7 %copy.33 = bf16[3072,768]{0,1:T(8,128)(2,1)} copy(bf16[3072,768]{1,0:T(8,128)(2,1)} %all-gather.13.cloned.1.call-done) | data formatting | bytes 9437184 | tf_op jit(solution)/shard_map/all_gather | solution.py:29
  286.7 9.6 %multiply_reduce_fusion = (f32[6,192]{1,0:T(8,128)S(1)}, f32[6,192,3072]{2,1,0:T(8,128)}) fusion(bf16[3072,6,128]{0,2,1:T(8,128)(2,1)} %bitcast.94, bf16[24,6,8,128]{3,2,1,0:T(8,128)(2,1)S(1)} %get-tuple-element.13), kind=kOutput, calls=%fused_computation.11 | convolution fusion | flops 913046400 | bytes 19173888 | tf_op jit(solution)/shard_map/qhd,khd->hqk/dot_general | solution.py:36
  296.3 7.5 %exponential_reduce_fusion = f32[6,192]{1,0:T(8,128)S(1)} fusion(f32[6,192,3072]{2,1,0:T(8,128)} %get-tuple-element.19, f32[6,192]{1,0:T(8,128)S(1)} %get-tuple-element.18), kind=kLoop, calls=%fused_computation.8 | loop fusion | flops 10615680 | bytes 14164992 | tf_op jit(solution)/shard_map/reduce_sum | solution.py:40
  303.8 8.5 %multiply_reduce_fusion.1 = (f32[192,6]{0,1:T(8,128)S(1)}, bf16[192,6,128]{2,0,1:T(8,128)(2,1)}) fusion(bf16[192,6,128]{2,1,0:T(8,128)(2,1)S(1)} %reshape_squeeze.3, bf16[3072,6,128]{0,2,1:T(8,128)(2,1)S(1)} %bitcast.103, f32[6,192,3072]{2,1,0:T(8,128)} %get-tuple-element.19, f32[6,192]{1,0:T(8,128)S(1)} %log_add_fusion), kind=kOutput, calls=%fused_computation.37 | convolution fusion | flops 917322624 | bytes 19473408 | tf_op jit(solution)/shard_map/hqk,khd->qhd/dot_general | solution.py:43
  312.3 20.3 %all-gather.2 = f32[16,192,6]{1,2,0:T(8,128)S(1)} all-gather(f32[1,192,6]{1,2,0:T(8,128)S(1)} %bitcast.108), channel_id=1, replica_groups=mesh['dp'=16,'seq'=16] {'seq'}, dimensions={0}, use_global_device_ids=true | all-gather | bytes 78336 | tf_op jit(solution)/shard_map/all_gather | solution.py:61
  332.8 20.5 %all-gather.1 = f32[16,192,6]{1,2,0:T(8,128)S(1)} all-gather(f32[1,192,6]{1,2,0:T(8,128)S(1)} %bitcast.107), channel_id=1, replica_groups=mesh['dp'=16,'seq'=16] {'seq'}, dimensions={0}, use_global_device_ids=true | all-gather | bytes 78336 | tf_op jit(solution)/shard_map/all_gather | solution.py:60
  353.5 10.7 %fusion.42 = bf16[6,24,8,128]{3,2,1,0:T(8,128)(2,1)S(1)} fusion(bf16[3072,6,128]{0,2,1:T(8,128)(2,1)} %bitcast.95, f32[6,192,3072]{2,1,0:T(8,128)} %get-tuple-element.19, f32[6,192]{1,0:T(8,128)S(1)} %bitcast.109, f32[6,192]{1,0:T(8,128)S(1)} %log_add_fusion, bf16[3072,6,128]{0,2,1:T(8,128)(2,1)} %bitcast.100, bf16[192,6,128]{2,1,0:T(8,128)(2,1)S(1)} %reshape_squeeze.3), kind=kOutput, calls=%fused_computation.33 | convolution fusion | flops 1833320448 | bytes 24192000 | tf_op jit(solution)/shard_map/hqk,khd->qhd/dot_general | solution.py:56
  364.3 6.7 %copy.43 = bf16[3072,768]{0,1:T(8,128)(2,1)} copy(bf16[3072,768]{1,0:T(8,128)(2,1)} %all-gather.15.cloned.1.call-done) | data formatting | bytes 9437184 | tf_op jit(solution)/shard_map/all_gather | solution.py:65
  371.0 9.4 %fusion.54 = f32[6,3072,192]{1,2,0:T(8,128)} fusion(bf16[3072,6,128]{0,2,1:T(8,128)(2,1)} %bitcast.96, bf16[24,6,8,128]{3,2,1,0:T(8,128)(2,1)S(1)} %get-tuple-element.14), kind=kOutput, calls=%fused_computation.43 | convolution fusion | flops 905969664 | bytes 19169280 | tf_op jit(solution)/shard_map/qhd,khd->hqk/dot_general | solution.py:70
  380.3 8.8 %fusion.36 = bf16[6,24,8,128]{3,2,1,0:T(8,128)(2,1)S(1)} fusion(bf16[3072,6,128]{0,2,1:T(8,128)(2,1)} %bitcast.98, f32[6,3072,192]{1,2,0:T(8,128)} %fusion.54, f32[6,3072]{1,0:T(8,128)S(1)} %bitcast.105), kind=kOutput, calls=%fused_computation.31 | convolution fusion | flops 916733952 | bytes 19243008 | tf_op jit(solution)/shard_map/hqk,qhd->khd/dot_general | solution.py:74
  389.1 10.9 %fusion.45 = bf16[6,24,8,128]{3,2,1,0:T(8,128)(2,1)S(1)} fusion(bf16[3072,6,128]{0,2,1:T(8,128)(2,1)} %bitcast.97, f32[6,3072,192]{1,2,0:T(8,128)} %fusion.54, f32[6,3072]{1,0:T(8,128)S(1)} %bitcast.104, f32[6,3072]{1,0:T(8,128)} %bitcast.106, bf16[3072,6,128]{0,2,1:T(8,128)(2,1)} %bitcast.99, bf16[24,6,8,128]{3,2,1,0:T(8,128)(2,1)S(1)} %get-tuple-element.12), kind=kOutput, calls=%fused_computation.34 | convolution fusion | flops 1833320448 | bytes 24330240 | tf_op jit(solution)/shard_map/hqk,qhd->khd/dot_general | solution.py:86
  400.1 5.0 fusion.6
  405.1 9.8 %copy.64 = bf16[1536,2304]{1,0:T(8,128)(2,1)} copy(bf16[1536,2304]{0,1:T(8,128)(2,1)} %fusion.6) | data formatting | bytes 14155776
  417.1 99.5 %reduce-scatter.4.cloned.1.call-done = bf16[96,2304]{1,0:T(8,128)(2,1)} async-done(((bf16[1536,2304]{1,0:T(8,128)(2,1)}), bf16[96,2304]{1,0:T(8,128)(2,1)}) %reduce-scatter.4.cloned.1.call-update) | async-done | bytes 442384
  516.7 2.1 copy.65
  518.8 6.3 fusion.23
  525.0 129.7 %all-reduce.2.cloned.1.call-done = bf16[96,2304]{0,1:T(8,128)(2,1)} async-done(((bf16[96,2304]{0,1:T(8,128)(2,1)}), bf16[96,2304]{0,1:T(8,128)(2,1)}) %all-reduce.2.cloned.1.call-update) | async-done | bytes 442384 | tf_op jit(solution)/shard_map/psum | solution.py:112
  (41 shorter events, 8.7 us)
Async XLA Ops:
  7.2 78.0 %copy-start = (bf16[1,192,1536]{2,1,0:T(8,128)(2,1)S(1)}, bf16[1,192,1536]{2,1,0:T(8,128)(2,1)}, u32[]{:S(2)}) copy-start(bf16[1,192,1536]{2,1,0:T(8,128)(2,1)} %param.3) | copy-start | bytes 1769476
  7.2 78.0 %all-gather.9.cloned.1.call-start = ((), (), s32[]{:S(2)}) async-start(), calls=%async_computation.1 | async-start | bytes 7520256 | tf_op jit(solution)/shard_map/all_gather | solution.py:20
  7.9 141.9 %all-gather.17.cloned.1.call-start = ((), (), s32[]{:S(2)}) async-start(), calls=%async_computation.6 | async-start | bytes 5013504 | tf_op jit(solution)/shard_map/all_gather | solution.py:66
  8.7 83.3 %copy-start.1 = (bf16[1,192,768]{2,1,0:T(8,128)(2,1)S(1)}, bf16[1,192,768]{2,1,0:T(8,128)(2,1)}, u32[]{:S(2)}) copy-start(bf16[1,192,768]{2,1,0:T(8,128)(2,1)} %param.5) | copy-start | bytes 884740
  8.7 206.3 %all-gather.11.cloned.1.call-start = ((), (), s32[]{:S(2)}) async-start(), calls=%async_computation.2 | async-start | bytes 5013504 | tf_op jit(solution)/shard_map/all_gather | solution.py:30
  90.8 189.2 %all-gather.13.cloned.1.call-start = ((), (), s32[]{:S(2)}) async-start(), calls=%async_computation.3 | async-start | bytes 5013504 | tf_op jit(solution)/shard_map/all_gather | solution.py:29
  91.3 272.9 %all-gather.15.cloned.1.call-start = ((), (), s32[]{:S(2)}) async-start(), calls=%async_computation.4 | async-start | bytes 5013504 | tf_op jit(solution)/shard_map/all_gather | solution.py:65
  91.9 424.7 %reduce-scatter.4.cloned.1.call-start = ((), (), s32[]{:S(2)}) async-start(), calls=%async_computation.7 | async-start | bytes 7520256
  280.0 23.8 %slice-start = ((s8[4718592]{0:T(1024)(128)(4,1)}), s8[524288]{0:T(1024)(128)(4,1)S(1)}, s32[]{:S(2)}) async-start(s8[4718592]{0:T(1024)(128)(4,1)} %bitcast.101), calls=%async_computation.8 | async-start | bytes 1048576
  286.7 17.1 %slice-start.1 = ((s8[4718592]{0:T(1024)(128)(4,1)}), s8[4194304]{0:T(1024)(128)(4,1)S(1)}, s32[]{:S(2)}) async-start(s8[4718592]{0:T(1024)(128)(4,1)} %bitcast.101), calls=%async_computation.9 | async-start | bytes 8388608
  353.5 26.9 %copy-start.3 = (f32[3072,6]{0,1:T(8,128)}, f32[3072,6]{0,1:T(8,128)S(1)}, u32[]{:S(2)}) copy-start(f32[3072,6]{0,1:T(8,128)S(1)} %reshape.59) | copy-start | bytes 221188
  414.9 1.0 copy-start.2
  414.9 239.8 %all-reduce.2.cloned.1.call-start = ((), (), s32[]{:S(2)}) async-start(), calls=%async_computation.5 | async-start | bytes 1179648 | tf_op jit(solution)/shard_map/psum | solution.py:112
Sparse Core Ops, SparseCore 0:
  10.7 74.4 all-gather.8
  87.9 61.8 all-gather.16
  153.1 61.8 all-gather.10
  218.1 61.8 all-gather.12
  283.1 62.3 all-gather.14
  415.0 101.5 reduce-scatter.3
  519.3 135.3 all-reduce.1
where the time goes:
time: 665 us; the launch traced here: 664 us
  waiting for transfers between devices  482 us (72%)
  matrix products  73.6 us (11%)
  local copies, waits for them, and re-layouts  44.6 us (7%)
  blocking collectives  40.9 us (6%)
  between operations  14.3 us (2%)
  other arithmetic  7.47 us (1%)
    psum x1, waiting for transfers between devices, on_device(): total = lax.psum(summed, 'dp').astype(jnp.float32)  130 us
    unnamed x8, waiting for transfers between devices  102 us
    all_gather x1, waiting for transfers between devices, on_device(): weights = lax.all_gather(w_qkv, 'seq', axis=0, tiled=True)  76.5 us
    all_gather x1, waiting for transfers between devices, on_device(): lax.all_gather(values_here, 'seq', axis=0, tiled=True)  58.5 us
    all_gather x1, waiting for transfers between devices, on_device(): lax.all_gather(keys_here, 'seq', axis=0, tiled=True)  58.3 us
    all_gather x1, waiting for transfers between devices, on_device(): lax.all_gather(grad_out, 'seq', axis=0, tiled=True)  57.5 us
    all_gather x1, blocking collectives, on_device(): lax.all_gather(log_total.T, 'seq', axis=0, tiled=True)  20.5 us
    all_gather x1, blocking collectives, on_device(): lax.all_gather(delta_rows, 'seq', axis=0, tiled=True)  20.3 us
  transfers between devices with their start and end apart: 7, of which 6 were waited for; matrix products, arithmetic and copies ran while one was open for 11% of the time, Pallas kernels for 0%

commit v1 on v0

v1 whole, which is shorter than its diff:
```python
import math

import jax
import jax.numpy as jnp
from jax import lax
from jax.experimental import pallas as pl
from jax.experimental.pallas import tpu as pltpu
from jax.sharding import PartitionSpec as P

MESH = pl.DeviceIdType.MESH
BF = jnp.bfloat16
F32 = jnp.float32
ROWS = 192
D = 1536
HEAD = 128
GROUP = 3
GW = GROUP * HEAD
WROWS = 96
HALF_SCALE = 1.0 / math.sqrt(HEAD)
LOG2E = 1.4426950408889634


class Place:
    def __init__(self):
        dp, seq = lax.axis_index("dp"), lax.axis_index("seq")
        self.z, self.yl = lax.rem(dp, 8), lax.div(dp, 8)
        self.c, self.yh, self.x = lax.rem(seq, 2), lax.rem(lax.div(seq, 2), 2), lax.div(seq, 4)

    def device(self, x=None, yh=None, c=None, yl=None, z=None):
        x = self.x if x is None else x
        yh = self.yh if yh is None else yh
        c = self.c if c is None else c
        yl = self.yl if yl is None else yl
        z = self.z if z is None else z
        return (yl * 8 + z, x * 4 + yh * 2 + c)

    def xs(self, dx):
        return lax.rem(self.x + (dx + 4), 4)


class Net:
    def __init__(self, send, recv, local):
        self.send, self.recv, self.local = send, recv, local
        self.n = 0
        self.m = 0
        self.all = []

    def go(self, src, dst, device):
        cp = pltpu.make_async_remote_copy(
            src_ref=src, dst_ref=dst, send_sem=self.send.at[self.n], recv_sem=self.recv.at[self.n],
            device_id=device, device_id_type=MESH,
        )
        self.n += 1
        cp.start()
        self.all.append(cp)
        return cp

    def here(self, src, dst):
        cp = pltpu.make_async_copy(src, dst, self.local.at[self.m])
        self.m += 1
        cp.start()
        return cp

    def drain(self):
        for cp in self.all:
            cp.wait_send()


def greet(devices):
    barrier = pltpu.get_barrier_semaphore()
    for device in devices:
        pl.semaphore_signal(barrier, inc=1, device_id=device, device_id_type=MESH)
    pl.semaphore_wait(barrier, len(devices))


def rows_of(start, size, unit):
    return pl.ds(pl.multiple_of(start, unit), size)


def gather_kernel(x_ref, w_ref, g_ref, x2, w2, g2, qkv, send, recv, local):
    p = Place()
    net = Net(send, recv, local)
    ypair = p.device(yh=1 - p.yh)
    mirror = p.device(yh=1 - p.yh, yl=1 - p.yl)
    right, left, sib = p.device(x=p.xs(1)), p.device(x=p.xs(-1)), p.device(c=1 - p.c)
    greet([ypair, mirror, right, left, sib])

    def wrows(x, yh):
        return w2.at[rows_of((x * 4 + yh * 2 + p.c) * WROWS, WROWS, 32)]

    def wcols(yh, j):
        return w_ref.at[:, rows_of(yh * GW + 2 * GW * j, GW, 128)]

    mine = wrows(p.x, p.yh)
    theirs = [net.go(wcols(1 - p.yh, j), mine.at[:, pl.ds(j * GW, GW)], mirror) for j in range(3)]
    own = [net.here(wcols(p.yh, j), mine.at[:, pl.ds(j * GW, GW)]) for j in range(3)]
    my_rows = rows_of(p.yh * ROWS, ROWS, 64)
    xo = net.go(x_ref, x2.at[my_rows], ypair)
    xl = net.here(x_ref, x2.at[my_rows])
    go = net.go(g_ref.at[:, rows_of((1 - p.yh) * GW, GW, 128)], g2.at[my_rows], ypair)
    gl = net.here(g_ref.at[:, rows_of(p.yh * GW, GW, 128)], g2.at[my_rows])
    for cp in own:
        cp.wait()
    a_right, a_left = net.go(mine, mine, right), net.go(mine, mine, left)
    relays = [net.go(mine, mine, sib)]

    def relay(x, yh):
        block = wrows(x, yh)
        relays.append(net.go(block, block, sib))

    for cp in theirs:
        cp.wait_recv()
    block = wrows(p.x, 1 - p.yh)
    b_right, b_left = net.go(block, block, right), net.go(block, block, left)
    relay(p.x, 1 - p.yh)
    a_right.wait_recv()
    block = wrows(p.xs(-1), p.yh)
    f_right = net.go(block, block, right)
    relay(p.xs(-1), p.yh)
    a_left.wait_recv()
    relay(p.xs(1), p.yh)
    b_left.wait_recv()
    block = wrows(p.xs(1), 1 - p.yh)
    f_left = net.go(block, block, left)
    relay(p.xs(1), 1 - p.yh)
    b_right.wait_recv()
    relay(p.xs(-1), 1 - p.yh)
    f_right.wait_recv()
    relay(p.xs(2), p.yh)
    f_left.wait_recv()
    relay(p.xs(2), 1 - p.yh)
    for cp in (xl, gl):
        cp.wait()
    for cp in (xo, go):
        cp.wait_recv()
    for cp in relays:
        cp.wait_recv()
    for j in range(3):
        cols = pl.ds(j * GW, GW)
        qkv[:, cols] = jnp.dot(x2[...], w2[:, cols], preferred_element_type=F32).astype(BF)
    net.drain()


NT = (((1,), (1,)), ((), ()))


def attention_kernel(qkv, g2, att, dproj, kv, part, other, sibl, land_a, land_b, land_l, land_r,
                     m_ref, l_ref, o_ref, lse_ref, delta_ref, dq_ref, o2, send, recv, local):
    p = Place()
    net = Net(send, recv, local)
    ypair = p.device(yh=1 - p.yh)
    right, left, sib = p.device(x=p.xs(1)), p.device(x=p.xs(-1)), p.device(c=1 - p.c)
    greet([ypair, right, left, sib])
    n = 2 * ROWS

    def block(x, half):
        return kv.at[rows_of(x * 2 * n + p.c * n + half * ROWS, ROWS, 64)]

    def relay(x, half):
        return net.go(block(x, half), block(x, half), sib)

    cps = [net.here(qkv.at[pl.ds(h * ROWS, ROWS), pl.ds(GW, 2 * GW)], block(p.x, h)) for h in range(2)]
    for cp in cps:
        cp.wait()
    a, b = block(p.x, 0), block(p.x, 1)
    a_right, b_left = net.go(a, a, right), net.go(b, b, left)
    b_right, a_left = net.go(b, b, right), net.go(a, a, left)
    relays = [relay(p.x, 0), relay(p.x, 1)]

    m_ref[...] = jnp.full_like(m_ref, -1e30)
    l_ref[...] = jnp.zeros_like(l_ref)
    o_ref[...] = jnp.zeros_like(o_ref)
    c2 = HALF_SCALE * LOG2E

    def load(x, h, which):
        return kv[rows_of(x * 2 * n, 2 * n, 128), pl.ds(which * GW + h * HEAD, HEAD)]

    def forward(x):
        for h in range(GROUP):
            q = qkv[:, pl.ds(h * HEAD, HEAD)]
            s = lax.dot_general(load(x, h, 0), q, NT, preferred_element_type=F32) * c2
            m_old = m_ref[pl.ds(h, 1), :]
            m_new = jnp.maximum(m_old, jnp.max(s, axis=0, keepdims=True))
            alpha = jnp.exp2(m_old - m_new)
            e = jnp.exp2(s - m_new)
            m_ref[pl.ds(h, 1), :] = m_new
            l_ref[pl.ds(h, 1), :] = l_ref[pl.ds(h, 1), :] * alpha + jnp.sum(e, axis=0, keepdims=True)
            hr = pl.ds(h * HEAD, HEAD)
            o_ref[hr, :] = o_ref[hr, :] * alpha + jnp.dot(
                load(x, h, 1).T, e.astype(BF), preferred_element_type=F32)

    for cp in relays:
        cp.wait_recv()
    forward(p.x)
    a_right.wait_recv()
    f_right = net.go(block(p.xs(-1), 0), block(p.xs(-1), 0), right)
    r0 = relay(p.xs(-1), 0)
    b_left.wait_recv()
    f_left = net.go(block(p.xs(1), 1), block(p.xs(1), 1), left)
    r1 = relay(p.xs(1), 1)
    b_right.wait_recv()
    r2 = relay(p.xs(-1), 1)
    a_left.wait_recv()
    r3 = relay(p.xs(1), 0)
    for cp in (r0, r2, r1, r3):
        cp.wait_recv()
    forward(p.xs(-1))
    forward(p.xs(1))
    f_right.wait_recv()
    r4 = relay(p.xs(2), 0)
    f_left.wait_recv()
    r5 = relay(p.xs(2), 1)
    r4.wait_recv()
    r5.wait_recv()
    forward(p.xs(2))

    for h in range(GROUP):
        hr = pl.ds(h * HEAD, HEAD)
        l = l_ref[pl.ds(h, 1), :]
        o = (o_ref[hr, :] / l).astype(BF)
        lse_ref[pl.ds(h, 1), :] = m_ref[pl.ds(h, 1), :] + jnp.log2(l)
        delta_ref[pl.ds(h, 1), :] = jnp.sum(
            o.astype(F32) * g2[:, hr].T.astype(F32), axis=0, keepdims=True)
        o2[:, hr] = o.T
    dq_ref[...] = jnp.zeros_like(dq_ref)
    cols = rows_of(p.yh * GW, GW, 128)
    ao = net.go(o2.at[rows_of((1 - p.yh) * ROWS, ROWS, 64)], att.at[:, cols], ypair)
    al = net.here(o2.at[rows_of(p.yh * ROWS, ROWS, 64)], att.at[:, cols])

    def backward(i, x):
        for h in range(GROUP):
            hr = pl.ds(h * HEAD, HEAD)
            q, g = qkv[:, hr], g2[:, hr]
            k = load(x, h, 0)
            s = lax.dot_general(k, q, NT, preferred_element_type=F32) * c2
            e = jnp.exp2(s - lse_ref[pl.ds(h, 1), :])
            dv = jnp.dot(e.astype(BF), g, preferred_element_type=F32).astype(BF)
            de = lax.dot_general(load(x, h, 1), g, NT, preferred_element_type=F32)
            ds = (e * (de - delta_ref[pl.ds(h, 1), :])).astype(BF)
            dk = (jnp.dot(ds, q, preferred_element_type=F32) * HALF_SCALE).astype(BF)
            dq_ref[hr, :] += jnp.dot(k.T, ds, preferred_element_type=F32)
            vr = pl.ds(GW + h * HEAD, HEAD)
            part[i, 0, :, hr] = dk[:n]
            part[i, 1, :, hr] = dk[n:]
            part[i, 0, :, vr] = dv[:n]
            part[i, 1, :, vr] = dv[n:]
        return net.go(part.at[i, 1 - p.c], sibl.at[i], sib)

    def add(i, rows, *lands):
        t = part[i, p.c, rows].astype(F32) + sibl[i, rows].astype(F32)
        for ref in lands:
            t = t + ref[...].astype(F32)
        return t

    top, bottom = pl.ds(0, ROWS), pl.ds(ROWS, ROWS)
    sb = backward(0, p.xs(2))
    sb.wait_recv()
    other[0] = add(0, pl.ds(0, n)).astype(BF)
    ga = net.go(other.at[0, top], land_a, right)
    gb = net.go(other.at[0, bottom], land_b, left)
    s1 = backward(1, p.xs(1))
    s2 = backward(2, p.xs(-1))
    s1.wait_recv()
    ga.wait_recv()
    other[1, top] = add(1, top, land_a).astype(BF)
    other[1, bottom] = add(1, bottom).astype(BF)
    gl = net.go(other.at[1], land_l, right)
    s2.wait_recv()
    gb.wait_recv()
    other[2, top] = add(2, top).astype(BF)
    other[2, bottom] = add(2, bottom, land_b).astype(BF)
    gr = net.go(other.at[2], land_r, left)
    s3 = backward(3, p.x)
    for h in range(GROUP):
        hr = pl.ds(h * HEAD, HEAD)
        dproj[:, hr] = (dq_ref[hr, :] * HALF_SCALE).astype(BF).T
    s3.wait_recv()
    gl.wait_recv()
    gr.wait_recv()
    dproj[:, pl.ds(GW, 2 * GW)] = add(3, pl.ds(0, n), land_l, land_r).astype(BF)
    al.wait()
    ao.wait_recv()
    net.drain()


def grad_kernel(x2, w2, dproj, gi, gw, part, other, sibl, land_a, land_b, land_l, land_r,
                gi_out, gi_in, y_out, y_in, zbuf, z_in, ybuf, fin, send, recv, local):
    p = Place()
    net = Net(send, recv, local)
    ypair = p.device(yh=1 - p.yh)
    right, left, sib = p.device(x=p.xs(1)), p.device(x=p.xs(-1)), p.device(c=1 - p.c)
    near = p.device(yl=1 - p.yl)
    mirror = p.device(yh=1 - p.yh, yl=1 - p.yl)
    zs = [lax.rem(p.z + d, 8) for d in range(8)]
    greet([ypair, right, left, sib, near, mirror] + [p.device(z=zs[d]) for d in range(1, 8)])

    def term(i, x):
        t = lax.dot_general(x2[:, rows_of(x * GW, GW, 128)], dproj[...], (((0,), (0,)), ((), ())),
                            preferred_element_type=F32).astype(BF)
        for c in range(2):
            for yh in range(2):
                lo = (yh * 2 + c) * WROWS
                part[i, c, yh] = t[lo:lo + WROWS]
        return net.go(part.at[i, 1 - p.c], sibl.at[i], sib)

    def add(i, yh, *lands):
        t = part[i, p.c, yh].astype(F32) + sibl[i, yh].astype(F32)
        for ref in lands:
            t = t + ref.astype(F32)
        return t

    sb = term(0, p.xs(2))
    s1 = term(1, p.xs(1))
    s2 = term(2, p.xs(-1))
    sb.wait_recv()
    for yh in range(2):
        other[0, yh] = add(0, yh).astype(BF)
    ga = net.go(other.at[0, 0], land_a, right)
    gb = net.go(other.at[0, 1], land_b, left)
    far = dproj[rows_of((1 - p.yh) * ROWS, ROWS, 64), :]
    gi_out[...] = lax.dot_general(far, w2[...], NT, preferred_element_type=F32).astype(BF)
    gx = net.go(gi_out, gi_in, ypair)
    s1.wait_recv()
    s2.wait_recv()
    other[1, 1] = add(1, 1).astype(BF)
    other[2, 0] = add(2, 0).astype(BF)
    ga.wait_recv()
    other[1, 0] = add(1, 0, land_a[...]).astype(BF)
    gl = net.go(other.at[1], land_l, right)
    gb.wait_recv()
    other[2, 1] = add(2, 1, land_b[...]).astype(BF)
    gr = net.go(other.at[2], land_r, left)
    s3 = term(3, p.x)
    near_rows = dproj[rows_of(p.yh * ROWS, ROWS, 64), :]
    part_gi = lax.dot_general(near_rows, w2[...], NT, preferred_element_type=F32)
    gx.wait_recv()
    gi[...] = (part_gi + gi_in[...].astype(F32)).astype(BF)
    s3.wait_recv()
    gl.wait_recv()
    gr.wait_recv()
    for yh in range(2):
        y_out[yh] = add(3, yh, land_l[yh], land_r[yh]).astype(BF)
    keep = lax.rem(p.yh + p.yl, 2)
    gy = net.go(y_out.at[1 - keep], y_in, near)
    gy.wait_recv()
    t = (y_out[keep].astype(F32) + y_in[...].astype(F32)).astype(BF)
    for j in range(9):
        zbuf[pl.ds(j * WROWS, WROWS), :] = t[:, j * 128:(j + 1) * 128]
    zbuf[pl.ds(864, 32), :] = jnp.zeros((32, 128), BF)
    zc = [net.go(zbuf.at[rows_of(zs[d] * 112, 112, 16)], z_in.at[d - 1], p.device(z=zs[d])) for d in range(1, 8)]
    t = zbuf[rows_of(p.z * 112, 112, 16), :].astype(F32)
    for d in range(1, 8):
        zc[d - 1].wait_recv()
        t = t + z_in[d - 1].astype(F32)
    ybuf[p.yh, p.yl] = t.astype(BF)
    me = ybuf.at[p.yh, p.yl]
    yc = [net.go(me, me, dev) for dev in (near, ypair, mirror)]
    for cp in yc:
        cp.wait_recv()
    zr = rows_of(p.z * 112, 112, 16)
    for g in range(2):
        fin[g, zr, :] = ybuf[g, lax.rem(p.yh + g, 2)]
    blk = fin.at[:, zr]
    fc = [net.go(blk, blk, p.device(z=zs[d])) for d in range(1, 8)]
    for cp in fc:
        cp.wait_recv()
    for g in range(2):
        for j in range(9):
            col = (j // 3) * 2 * GW + g * GW + (j % 3) * 128
            gw[:, pl.ds(col, 128)] = fin[g, pl.ds(j * WROWS, WROWS), :]
    net.drain()


VMEM = pl.BlockSpec(memory_space=pltpu.VMEM)


def call(kernel, cid, args, outs, scratch, copies, local):
    return pl.pallas_call(
        kernel,
        out_shape=[jax.ShapeDtypeStruct(s, BF) for s in outs],
        in_specs=[VMEM] * len(args),
        out_specs=[VMEM] * len(outs),
        scratch_shapes=[pltpu.VMEM(s, t) for s, t in scratch] + [
            pltpu.SemaphoreType.DMA((copies,)), pltpu.SemaphoreType.DMA((copies,)),
            pltpu.SemaphoreType.DMA((local,))],
        compiler_params=pltpu.CompilerParams(
            collective_id=cid, has_side_effects=True, vmem_limit_bytes=56 * 2**20),
    )(*args)


def on_device(seq_embed, w_qkv, upstream):
    n = 2 * ROWS
    x2, w2, g2, qkv = call(
        gather_kernel, 0, (seq_embed[0], w_qkv, upstream[0]),
        [(n, D), (D, 3 * GW), (n, GW), (n, 3 * GW)], [], 24, 8)
    kvw = 2 * GW
    att, dproj = call(
        attention_kernel, 1, (qkv, g2), [(ROWS, 2 * GW), (n, 3 * GW)],
        [((8 * n, kvw), BF), ((4, 2, n, kvw), BF), ((3, n, kvw), BF), ((4, n, kvw), BF),
         ((ROWS, kvw), BF), ((ROWS, kvw), BF), ((n, kvw), BF), ((n, kvw), BF),
         ((8, n), F32), ((8, n), F32), ((GW, n), F32), ((8, n), F32), ((8, n), F32), ((GW, n), F32),
         ((n, GW), BF)], 24, 4)
    gcol = 3 * GW
    gi, gw = call(
        grad_kernel, 2, (x2, w2, dproj), [(ROWS, D), (WROWS, 6 * GW)],
        [((4, 2, 2, WROWS, gcol), BF), ((3, 2, WROWS, gcol), BF), ((4, 2, WROWS, gcol), BF),
         ((WROWS, gcol), BF), ((WROWS, gcol), BF), ((2, WROWS, gcol), BF), ((2, WROWS, gcol), BF),
         ((ROWS, D), BF), ((ROWS, D), BF), ((2, WROWS, gcol), BF), ((WROWS, gcol), BF),
         ((896, 128), BF), ((7, 112, 128), BF), ((2, 2, 112, 128), BF), ((2, 896, 128), BF)], 32, 4)
    return att[None], gi[None], gw


def solution(mesh):
    placed = (P("dp", "seq", None), P("seq", None), P("dp", "seq", None))
    return jax.shard_map(
        on_device,
        mesh=mesh,
        in_specs=placed,
        out_specs=(P("dp", "seq", None), P("dp", "seq", None), P("seq", None)),
        check_vma=False,
    )
```

time: 665 us -> 170 us (0.26)
  waiting for transfers between devices: 482 us -> 0 us
  Pallas kernels: 0 us -> 165 us
  matrix products: 73.6 us -> 0 us
  blocking collectives: 40.9 us -> 0 us
  local copies, waits for them, and re-layouts: 44.6 us -> 4.44 us
  between operations: 14.3 us -> 0.67 us
  other arithmetic: 7.47 us -> 0 us
    all_gather x5 -> x0, waiting for transfers between devices: 251 us -> none  [the longest x1 76.5 us: on_device(): weights = lax.all_gather(w_qkv, 'seq', axis=0, tiled=True)]
    pallas_call x0 -> x3, Pallas kernels: none -> 165 us  [call(): pl.pallas_call(kernel, out_shape=[jax.ShapeDtypeStruct(s, BF) for s in ou...]
    psum x1 -> x0, waiting for transfers between devices: 130 us -> none  [on_device(): total = lax.psum(summed, 'dp').astype(jnp.float32)]
    unnamed x8 -> x0, waiting for transfers between devices: 102 us -> none
    dot_general x9 -> x0, matrix products: 73.6 us -> none  [the longest x1 10.9 us: on_device(): jnp.einsum('hqk,qhd->khd', piece_grad_scores, query_piece, preferred_elem...]
    all_gather x2 -> x0, blocking collectives: 40.9 us -> none  [the longest x1 20.5 us: on_device(): lax.all_gather(log_total.T, 'seq', axis=0, tiled=True)]
    all_gather x6 -> x0, local copies, waits for them, and re-layouts: 26.8 us -> none  [the longest x1 6.72 us: on_device(): lax.all_gather(keys_here, 'seq', axis=0, tiled=True)]
    unnamed x20 -> x5, local copies, waits for them, and re-layouts: 16.1 us -> 4.44 us
  transfers between devices with their start and end apart: 7 -> 0, of which waited for: 6 -> 0; matrix products, arithmetic and copies ran while one was open for 11% -> 0% of each run, Pallas kernels for 0% -> 0%
where the time goes in v1:
time: 170 us
  Pallas kernels  165 us (97%)
  local copies, waits for them, and re-layouts  4.44 us (3%)
    pallas_call x3, Pallas kernels, call(): pl.pallas_call(kernel, out_shape=[jax.ShapeDtypeStruct(s, BF) for s in ou...  165 us
    unnamed x5, local copies, waits for them, and re-layouts  4.44 us

profile of v1, /device:TPU:2, one launch (start us, length us, event | category | flops | bytes accessed | tf_op | source)
XLA Modules:
  0.0 169.9 jit_solution(5584509503862730665)
XLA Ops:
  0.6 45.0 %shard_map.58 = (bf16[384,1536]{1,0:T(8,128)(2,1)}, bf16[1536,1152]{1,0:T(8,128)(2,1)}, bf16[384,384]{1,0:T(8,128)(2,1)}, bf16[384,1152]{1,0:T(8,128)(2,1)}) custom-call(bf16[192,1536]{1,0:T(8,128)(2,1)} %bitcast.5, bf16[96,2304]{1,0:T(8,128)(2,1)} %w_ref.1, bf16[192,768]{1,0:T(8,128)(2,1)} %bitcast.7), custom_call_target="tpu_custom_call" | custom-call | tf_op jit(solution)/shard_map/pallas_call | solution.py:378
  45.6 57.8 %shard_map.59 = (bf16[192,768]{1,0:T(8,128)(2,1)}, bf16[384,1152]{1,0:T(8,128)(2,1)}) custom-call(bf16[384,1152]{1,0:T(8,128)(2,1)} %get-tuple-element.11.qkv, bf16[384,384]{1,0:T(8,128)(2,1)} %get-tuple-element.12.g2), custom_call_target="tpu_custom_call" | custom-call | tf_op jit(solution)/shard_map/pallas_call | solution.py:378
  103.4 0.0 copy-start
  103.4 62.1 %shard_map.60 = (bf16[192,1536]{1,0:T(8,128)(2,1)}, bf16[96,2304]{1,0:T(8,128)(2,1)}) custom-call(bf16[384,1536]{1,0:T(8,128)(2,1)} %get-tuple-element.14.x2, bf16[1536,1152]{1,0:T(8,128)(2,1)} %get-tuple-element.15.w2, bf16[384,1152]{1,0:T(8,128)(2,1)} %get-tuple-element.16.dproj), custom_call_target="tpu_custom_call" | custom-call | tf_op jit(solution)/shard_map/pallas_call | solution.py:378
  165.5 0.0 copy-done
  165.5 0.7 copy.9
  166.2 1.9 %copy.10 = bf16[1,192,1536]{2,1,0:T(8,128)(2,1)} copy(bf16[1,192,1536]{2,1,0:T(8,128)(2,1)} %bitcast.4) | data formatting | bytes 1179648
  168.1 1.8 %copy.11 = bf16[96,2304]{1,0:T(8,128)(2,1)} copy(bf16[96,2304]{1,0:T(8,128)(2,1)} %get-tuple-element.24) | data formatting | bytes 884736
Async XLA Ops:
  103.4 62.1 %copy-start = (bf16[192,768]{1,0:T(8,128)(2,1)S(1)}, bf16[192,768]{1,0:T(8,128)(2,1)}, u32[]{:S(2)}) copy-start(bf16[192,768]{1,0:T(8,128)(2,1)} %get-tuple-element.13) | copy-start | bytes 884740

commit v2 on v1

v2 whole, which is shorter than its diff:
```python
import math

import jax
import jax.numpy as jnp
from jax import lax
from jax.experimental import pallas as pl
from jax.experimental.pallas import tpu as pltpu
from jax.sharding import PartitionSpec as P

MESH = pl.DeviceIdType.MESH
BF = jnp.bfloat16
F32 = jnp.float32
ROWS = 192
D = 1536
HEAD = 128
GROUP = 3
GW = GROUP * HEAD
WROWS = 96
HALF_SCALE = 1.0 / math.sqrt(HEAD)
LOG2E = 1.4426950408889634


class Place:
    def __init__(self):
        dp, seq = lax.axis_index("dp"), lax.axis_index("seq")
        self.z, self.yl = lax.rem(dp, 8), lax.div(dp, 8)
        self.c, self.yh, self.x = lax.rem(seq, 2), lax.rem(lax.div(seq, 2), 2), lax.div(seq, 4)

    def device(self, x=None, yh=None, c=None, yl=None, z=None):
        x = self.x if x is None else x
        yh = self.yh if yh is None else yh
        c = self.c if c is None else c
        yl = self.yl if yl is None else yl
        z = self.z if z is None else z
        return (yl * 8 + z, x * 4 + yh * 2 + c)

    def xs(self, dx):
        return lax.rem(self.x + (dx + 4), 4)


class Net:
    def __init__(self, send, recv, local):
        self.send, self.recv, self.local = send, recv, local
        self.n = 0
        self.m = 0
        self.all = []

    def go(self, src, dst, device):
        cp = pltpu.make_async_remote_copy(
            src_ref=src, dst_ref=dst, send_sem=self.send.at[self.n], recv_sem=self.recv.at[self.n],
            device_id=device, device_id_type=MESH,
        )
        self.n += 1
        cp.start()
        self.all.append(cp)
        return cp

    def here(self, src, dst):
        cp = pltpu.make_async_copy(src, dst, self.local.at[self.m])
        self.m += 1
        cp.start()
        return cp

    def drain(self):
        for cp in self.all:
            cp.wait_send()


def greet(devices):
    barrier = pltpu.get_barrier_semaphore()
    for device in devices:
        pl.semaphore_signal(barrier, inc=1, device_id=device, device_id_type=MESH)
    pl.semaphore_wait(barrier, len(devices))


def rows_of(start, size, unit):
    return pl.ds(pl.multiple_of(start, unit), size)


NT = (((1,), (1,)), ((), ()))
TN = (((0,), (0,)), ((), ()))
N = 2 * ROWS
GC = 3 * GW
KW = 2 * GW


def step_kernel(x_ref, w_ref, g_ref, att, gi, gw,
                x2, w2, qg, kv, m_ref, l_ref, o_ref, stat_out, stat_in, lse_ref, delta_ref,
                o_out, o_in, o2, dq_ref, dq_out, dq_in, kpart, kother, ksib, kland, dproj,
                part, other, sibl, land_a, land_b, land_l, land_r,
                gi_out, gi_in, y_out, y_in, zbuf, z_in, ybuf, fin, send, recv, local):
    p = Place()
    net = Net(send, recv, local)
    ypair = p.device(yh=1 - p.yh)
    mirror = p.device(yh=1 - p.yh, yl=1 - p.yl)
    near = p.device(yl=1 - p.yl)
    right, left, sib = p.device(x=p.xs(1)), p.device(x=p.xs(-1)), p.device(c=1 - p.c)
    odd = lax.rem(p.x, 2)
    qpair, kpair = p.device(x=p.xs(1 - 2 * odd)), p.device(x=p.xs(2 * odd - 1))
    zs = [lax.rem(p.z + d, 8) for d in range(8)]
    greet([ypair, mirror, near, right, left, sib] + [p.device(z=zs[d]) for d in range(1, 8)])

    def wrows(x, yh):
        return w2.at[rows_of((x * 4 + yh * 2 + p.c) * WROWS, WROWS, 32)]

    def wcols(yh, j):
        return w_ref.at[:, rows_of(yh * GW + 2 * GW * j, GW, 128)]

    mine = wrows(p.x, p.yh)
    theirs = [net.go(wcols(1 - p.yh, j), mine.at[:, pl.ds(j * GW, GW)], mirror) for j in range(3)]
    own = [net.here(wcols(p.yh, j), mine.at[:, pl.ds(j * GW, GW)]) for j in range(3)]
    my_rows = rows_of(p.yh * ROWS, ROWS, 64)
    far_rows = rows_of((1 - p.yh) * ROWS, ROWS, 64)
    for cp in own:
        cp.wait()
    a_right, a_left = net.go(mine, mine, right), net.go(mine, mine, left)
    relays = [net.go(mine, mine, sib)]

    def relay(x, yh):
        block = wrows(x, yh)
        relays.append(net.go(block, block, sib))

    qg[my_rows, pl.ds(GW, GW)] = g_ref[:, rows_of(p.yh * GW, GW, 128)]
    for cp in theirs:
        cp.wait_recv()
    xo = net.go(x_ref, x2.at[my_rows], ypair)
    block = wrows(p.x, 1 - p.yh)
    b_right, b_left = net.go(block, block, right), net.go(block, block, left)
    relay(p.x, 1 - p.yh)
    a_right.wait_recv()
    block = wrows(p.xs(-1), p.yh)
    f_right = net.go(block, block, right)
    relay(p.xs(-1), p.yh)
    a_left.wait_recv()
    relay(p.xs(1), p.yh)
    b_left.wait_recv()
    block = wrows(p.xs(1), 1 - p.yh)
    f_left = net.go(block, block, left)
    relay(p.xs(1), 1 - p.yh)
    b_right.wait_recv()
    relay(p.xs(-1), 1 - p.yh)
    go = net.go(g_ref.at[:, rows_of((1 - p.yh) * GW, GW, 128)], qg.at[my_rows, pl.ds(GW, GW)], ypair)
    f_right.wait_recv()
    relay(p.xs(2), p.yh)
    f_left.wait_recv()
    relay(p.xs(2), 1 - p.yh)
    for cp in relays:
        cp.wait_recv()

    def project(tokens, rows, j):
        t = jnp.dot(tokens[...], w2[:, pl.ds(j * GW, GW)], preferred_element_type=F32).astype(BF)
        if j == 0:
            qg[rows, pl.ds(0, GW)] = t
        else:
            kv[0, p.c, rows, pl.ds((j - 1) * GW, GW)] = t

    def give(rows):
        mk, mq = kv.at[0, p.c, rows], qg.at[rows]
        out = [net.go(mk, kv.at[1, p.c, rows], kpair), net.go(mk, mk, sib)]
        return out, mq

    project(x_ref, my_rows, 1)
    project(x_ref, my_rows, 2)
    (k_a, s_a), mq = give(my_rows)
    project(x_ref, my_rows, 0)
    there = rows_of(N + p.yh * ROWS, ROWS, 64)
    q_a = net.go(mq, qg.at[there], qpair)
    xo.wait_recv()
    far_x = x2.at[far_rows]
    project(far_x, far_rows, 1)
    project(far_x, far_rows, 2)
    (k_b, s_b), mq = give(far_rows)
    project(far_x, far_rows, 0)
    go.wait_recv()
    q_b = net.go(mq, qg.at[rows_of(N + (1 - p.yh) * ROWS, ROWS, 64)], qpair)
    x2[my_rows, :] = x_ref[...]

    m_ref[...] = jnp.full_like(m_ref, -1e30)
    l_ref[...] = jnp.zeros_like(l_ref)
    o_ref[...] = jnp.zeros_like(o_ref)
    c2 = HALF_SCALE * LOG2E

    def load(b, h, which):
        return kv[b, :, :, pl.ds(which * GW + h * HEAD, HEAD)].reshape(2 * N, HEAD)

    def forward(b, lo, size):
        qr = pl.ds(lo, size)
        for h in range(GROUP):
            q = qg[qr, pl.ds(h * HEAD, HEAD)]
            s = lax.dot_general(load(b, h, 0), q, NT, preferred_element_type=F32) * c2
            hs, hr = pl.ds(h, 1), pl.ds(h * HEAD, HEAD)
            m_old = m_ref[hs, qr]
            m_new = jnp.maximum(m_old, jnp.max(s, axis=0, keepdims=True))
            alpha = jnp.exp2(m_old - m_new)
            e = jnp.exp2(s - m_new)
            m_ref[hs, qr] = m_new
            l_ref[hs, qr] = l_ref[hs, qr] * alpha + jnp.sum(e, axis=0, keepdims=True)
            o_ref[hr, qr] = o_ref[hr, qr] * alpha + jnp.dot(
                load(b, h, 1).T, e.astype(BF), preferred_element_type=F32)

    s_a.wait_recv()
    s_b.wait_recv()
    forward(0, 0, N)
    k_a.wait_recv()
    t_a = net.go(kv.at[1, p.c, my_rows], kv.at[1, p.c, my_rows], sib)
    q_a.wait_recv()
    q_b.wait_recv()
    forward(0, N, N)
    k_b.wait_recv()
    t_b = net.go(kv.at[1, p.c, far_rows], kv.at[1, p.c, far_rows], sib)
    t_a.wait_recv()
    t_b.wait_recv()
    forward(1, 0, 2 * N)

    stat_out[...] = jnp.zeros_like(stat_out)
    for h in range(GROUP):
        hr = pl.ds(h * HEAD, HEAD)
        stat_out[pl.ds(h, 1), :] = m_ref[pl.ds(h, 1), :]
        stat_out[pl.ds(GROUP + h, 1), :] = l_ref[pl.ds(h, 1), :]
        stat_out[pl.ds(2 * GROUP + h, 1), :] = jnp.sum(
            o_ref[hr, :] * qg[:, pl.ds(GW + h * HEAD, HEAD)].T.astype(F32), axis=0, keepdims=True)
    st = net.go(stat_out, stat_in, qpair)
    st.wait_recv()

    def stat(i):
        other_half = stat_in[pl.ds(i, 1), :]
        return stat_out[pl.ds(i, 1), :], jnp.concatenate([other_half[:, N:], other_half[:, :N]], axis=1)

    for h in range(GROUP):
        hs = pl.ds(h, 1)
        m1, m2 = stat(h)
        l1, l2 = stat(GROUP + h)
        d1, d2 = stat(2 * GROUP + h)
        m = jnp.maximum(m1, m2)
        f1, f2 = jnp.exp2(m1 - m), jnp.exp2(m2 - m)
        l = l1 * f1 + l2 * f2
        lse_ref[hs, :] = m + jnp.log2(l)
        delta_ref[hs, :] = (d1 * f1 + d2 * f2) / l
        l_ref[hs, :] = f1 / l
    dq_ref[...] = jnp.zeros_like(dq_ref)

    def backward(i, b, h):
        hr = pl.ds(h * HEAD, HEAD)
        q, g = qg[:, hr], qg[:, pl.ds(GW + h * HEAD, HEAD)]
        k = load(b, h, 0)
        s = lax.dot_general(k, q, NT, preferred_element_type=F32) * c2
        e = jnp.exp2(s - lse_ref[pl.ds(h, 1), :])
        dv = jnp.dot(e.astype(BF), g, preferred_element_type=F32).astype(BF)
        de = lax.dot_general(load(b, h, 1), g, NT, preferred_element_type=F32)
        ds = (e * (de - delta_ref[pl.ds(h, 1), :])).astype(BF)
        dk = (jnp.dot(ds, q, preferred_element_type=F32) * HALF_SCALE).astype(BF)
        dq_ref[hr, :] += jnp.dot(k.T, ds, preferred_element_type=F32)
        for c in range(2):
            kpart[i, h, c, :, pl.ds(0, HEAD)] = dk[c * N:(c + 1) * N]
            kpart[i, h, c, :, pl.ds(HEAD, HEAD)] = dv[c * N:(c + 1) * N]
        return net.go(kpart.at[i, h, 1 - p.c], ksib.at[i, h], sib)

    def pass_on(h, cp):
        cp.wait_recv()
        kother[h] = (kpart[0, h, p.c].astype(F32) + ksib[0, h].astype(F32)).astype(BF)
        return net.go(kother.at[h], kland.at[h], kpair)

    k0 = backward(0, 1, 0)
    k1 = backward(0, 1, 1)
    lands = [pass_on(0, k0)]
    k2 = backward(0, 1, 2)
    lands.append(pass_on(1, k1))
    for h in range(GROUP):
        hr = pl.ds(h * HEAD, HEAD)
        o_ref[hr, :] = o_ref[hr, :] * l_ref[pl.ds(h, 1), :]
        o_out[hr, :] = o_ref[hr, pl.ds(N, N)].astype(BF)
    oc = net.go(o_out, o_in, qpair)
    lands.append(pass_on(2, k2))
    own_k, dqs = [], []
    for h in range(GROUP):
        hr = pl.ds(h * HEAD, HEAD)
        own_k.append(backward(1, 0, h))
        dq_out[hr, :] = (dq_ref[hr, pl.ds(N, N)] * HALF_SCALE).astype(BF)
        dqs.append(net.go(dq_out.at[hr], dq_in.at[hr], qpair))
    oc.wait_recv()
    for h in range(GROUP):
        hr = pl.ds(h * HEAD, HEAD)
        o2[:, hr] = (o_ref[hr, pl.ds(0, N)] + o_in[hr, :].astype(F32)).astype(BF).T
    cols = rows_of(p.yh * GW, GW, 128)
    ao = net.go(o2.at[far_rows], att.at[:, cols], ypair)
    al = net.here(o2.at[my_rows], att.at[:, cols])
    for h in range(GROUP):
        hr = pl.ds(h * HEAD, HEAD)
        dqs[h].wait_recv()
        dproj[:, hr] = (dq_ref[hr, pl.ds(0, N)] * HALF_SCALE + dq_in[hr, :].astype(F32)).astype(BF).T
    for h in range(GROUP):
        own_k[h].wait_recv()
        lands[h].wait_recv()
        t = kpart[1, h, p.c].astype(F32) + ksib[1, h].astype(F32) + kland[h].astype(F32)
        dproj[:, pl.ds(GW + h * HEAD, HEAD)] = t[:, :HEAD].astype(BF)
        dproj[:, pl.ds(2 * GW + h * HEAD, HEAD)] = t[:, HEAD:].astype(BF)

    def term(i, x):
        t = lax.dot_general(x2[:, rows_of(x * GW, GW, 128)], dproj[...], (((0,), (0,)), ((), ())),
                            preferred_element_type=F32).astype(BF)
        for c in range(2):
            for yh in range(2):
                lo = (yh * 2 + c) * WROWS
                part[i, c, yh] = t[lo:lo + WROWS]
        return net.go(part.at[i, 1 - p.c], sibl.at[i], sib)

    def add(i, yh, *lands):
        t = part[i, p.c, yh].astype(F32) + sibl[i, yh].astype(F32)
        for ref in lands:
            t = t + ref.astype(F32)
        return t

    sb = term(0, p.xs(2))
    s1 = term(1, p.xs(1))
    s2 = term(2, p.xs(-1))
    sb.wait_recv()
    for yh in range(2):
        other[0, yh] = add(0, yh).astype(BF)
    ga = net.go(other.at[0, 0], land_a, right)
    gb = net.go(other.at[0, 1], land_b, left)
    far = dproj[far_rows, :]
    gi_out[...] = lax.dot_general(far, w2[...], NT, preferred_element_type=F32).astype(BF)
    gx = net.go(gi_out, gi_in, ypair)
    s1.wait_recv()
    s2.wait_recv()
    other[1, 1] = add(1, 1).astype(BF)
    other[2, 0] = add(2, 0).astype(BF)
    ga.wait_recv()
    other[1, 0] = add(1, 0, land_a[...]).astype(BF)
    gl = net.go(other.at[1], land_l, right)
    gb.wait_recv()
    other[2, 1] = add(2, 1, land_b[...]).astype(BF)
    gr = net.go(other.at[2], land_r, left)
    s3 = term(3, p.x)
    near_rows = dproj[my_rows, :]
    part_gi = lax.dot_general(near_rows, w2[...], NT, preferred_element_type=F32)
    gx.wait_recv()
    gi[...] = (part_gi + gi_in[...].astype(F32)).astype(BF)
    s3.wait_recv()
    gl.wait_recv()
    gr.wait_recv()
    for yh in range(2):
        y_out[yh] = add(3, yh, land_l[yh], land_r[yh]).astype(BF)
    keep = lax.rem(p.yh + p.yl, 2)
    gy = net.go(y_out.at[1 - keep], y_in, near)
    gy.wait_recv()
    t = (y_out[keep].astype(F32) + y_in[...].astype(F32)).astype(BF)
    for j in range(9):
        zbuf[pl.ds(j * WROWS, WROWS), :] = t[:, j * 128:(j + 1) * 128]
    zbuf[pl.ds(864, 32), :] = jnp.zeros((32, 128), BF)
    zc = [net.go(zbuf.at[rows_of(zs[d] * 112, 112, 16)], z_in.at[d - 1], p.device(z=zs[d])) for d in range(1, 8)]
    t = zbuf[rows_of(p.z * 112, 112, 16), :].astype(F32)
    for d in range(1, 8):
        zc[d - 1].wait_recv()
        t = t + z_in[d - 1].astype(F32)
    ybuf[p.yh, p.yl] = t.astype(BF)
    me = ybuf.at[p.yh, p.yl]
    yc = [net.go(me, me, dev) for dev in (near, ypair, mirror)]
    for cp in yc:
        cp.wait_recv()
    zr = rows_of(p.z * 112, 112, 16)
    for g in range(2):
        fin[g, zr, :] = ybuf[g, lax.rem(p.yh + g, 2)]
    blk = fin.at[:, zr]
    fc = [net.go(blk, blk, p.device(z=zs[d])) for d in range(1, 8)]
    for cp in fc:
        cp.wait_recv()
    for g in range(2):
        for j in range(9):
            col = (j // 3) * 2 * GW + g * GW + (j % 3) * 128
            gw[:, pl.ds(col, 128)] = fin[g, pl.ds(j * WROWS, WROWS), :]
    al.wait()
    ao.wait_recv()
    net.drain()


VMEM = pl.BlockSpec(memory_space=pltpu.VMEM)


def on_device(seq_embed, w_qkv, upstream):
    scratch = [
        ((N, D), BF), ((D, GC), BF), ((2 * N, KW), BF), ((2, 2, N, KW), BF),
        ((8, 2 * N), F32), ((8, 2 * N), F32), ((GW, 2 * N), F32), ((16, 2 * N), F32), ((16, 2 * N), F32),
        ((8, 2 * N), F32), ((8, 2 * N), F32),
        ((GW, N), BF), ((GW, N), BF), ((N, GW), BF), ((GW, 2 * N), F32), ((GW, N), BF), ((GW, N), BF),
        ((2, GROUP, 2, N, 2 * HEAD), BF), ((GROUP, N, 2 * HEAD), BF), ((2, GROUP, N, 2 * HEAD), BF),
        ((GROUP, N, 2 * HEAD), BF), ((N, GC), BF),
        ((4, 2, 2, WROWS, GC), BF), ((3, 2, WROWS, GC), BF), ((4, 2, WROWS, GC), BF),
        ((WROWS, GC), BF), ((WROWS, GC), BF), ((2, WROWS, GC), BF), ((2, WROWS, GC), BF),
        ((ROWS, D), BF), ((ROWS, D), BF), ((2, WROWS, GC), BF), ((WROWS, GC), BF),
        ((896, 128), BF), ((7, 112, 128), BF), ((2, 2, 112, 128), BF), ((2, 896, 128), BF),
    ]
    copies = 80
    att, gi, gw = pl.pallas_call(
        step_kernel,
        out_shape=[jax.ShapeDtypeStruct(s, BF) for s in ((ROWS, KW), (ROWS, D), (WROWS, 2 * GC))],
        in_specs=[VMEM] * 3,
        out_specs=[VMEM] * 3,
        scratch_shapes=[pltpu.VMEM(s, t) for s, t in scratch] + [
            pltpu.SemaphoreType.DMA((copies,)), pltpu.SemaphoreType.DMA((copies,)),
            pltpu.SemaphoreType.DMA((8,))],
        compiler_params=pltpu.CompilerParams(
            collective_id=0, has_side_effects=True, vmem_limit_bytes=58 * 2**20),
    )(seq_embed[0], w_qkv, upstream[0])
    return att[None], gi[None], gw


def solution(mesh):
    placed = (P("dp", "seq", None), P("seq", None), P("dp", "seq", None))
    return jax.shard_map(
        on_device,
        mesh=mesh,
        in_specs=placed,
        out_specs=(P("dp", "seq", None), P("dp", "seq", None), P("seq", None)),
        check_vma=False,
    )
```

time: 170 us -> 131 us (0.77)
  Pallas kernels: 165 us -> 127 us
    pallas_call x3 -> x1, Pallas kernels: 165 us -> 127 us  [on_device(): pl.pallas_call(step_kernel, out_shape=[jax.ShapeDtypeStruct(s, BF) for s...]
    unnamed x5 -> x7, local copies, waits for them, and re-layouts: 4.44 us -> 3.75 us
where the time goes in v2:
time: 131 us
  Pallas kernels  127 us (97%)
  local copies, waits for them, and re-layouts  3.75 us (3%)
    pallas_call x1, Pallas kernels, on_device(): pl.pallas_call(step_kernel, out_shape=[jax.ShapeDtypeStruct(s, BF) for s...  127 us
    unnamed x7, local copies, waits for them, and re-layouts  3.75 us

profile of v2, /device:TPU:2, one launch (start us, length us, event | category | flops | bytes accessed | tf_op | source)
XLA Modules:
  0.0 131.1 jit_solution(1554669807743658083)
XLA Ops:
  0.6 126.7 %shard_map.58 = (bf16[192,768]{1,0:T(8,128)(2,1)}, bf16[192,1536]{1,0:T(8,128)(2,1)}, bf16[96,2304]{1,0:T(8,128)(2,1)}) custom-call(bf16[192,1536]{1,0:T(8,128)(2,1)} %bitcast.5, bf16[96,2304]{1,0:T(8,128)(2,1)} %w_ref.1, bf16[192,768]{1,0:T(8,128)(2,1)} %bitcast.7), custom_call_target="tpu_custom_call" | custom-call | tf_op jit(solution)/shard_map/pallas_call | solution.py:394
  127.4 0.0 copy-start
  127.4 1.8 %copy.9 = bf16[1,192,768]{2,1,0:T(8,128)(2,1)} copy(bf16[1,192,768]{2,1,0:T(8,128)(2,1)} %bitcast.6) | data formatting | bytes 589824
  129.1 0.0 copy-done
  129.1 0.0 copy-start.1
  129.1 0.8 copy.10
  130.0 0.4 copy-done.1
  130.4 0.8 copy.11
Async XLA Ops:
  127.4 1.8 %copy-start = (bf16[192,1536]{1,0:T(8,128)(2,1)S(1)}, bf16[192,1536]{1,0:T(8,128)(2,1)}, u32[]{:S(2)}) copy-start(bf16[192,1536]{1,0:T(8,128)(2,1)} %get-tuple-element.7) | copy-start | bytes 1769476
  129.1 1.2 copy-start.1

commit v3 on v2

v3 whole, which is shorter than its diff:
```python
import math

import jax
import jax.numpy as jnp
from jax import lax
from jax.experimental import pallas as pl
from jax.experimental.pallas import tpu as pltpu
from jax.sharding import PartitionSpec as P

MESH = pl.DeviceIdType.MESH
BF = jnp.bfloat16
F32 = jnp.float32
ROWS = 192
D = 1536
HEAD = 128
GROUP = 3
GW = GROUP * HEAD
WROWS = 96
HALF_SCALE = 1.0 / math.sqrt(HEAD)
LOG2E = 1.4426950408889634


class Place:
    def __init__(self):
        dp, seq = lax.axis_index("dp"), lax.axis_index("seq")
        self.z, self.yl = lax.rem(dp, 8), lax.div(dp, 8)
        self.c, self.yh, self.x = lax.rem(seq, 2), lax.rem(lax.div(seq, 2), 2), lax.div(seq, 4)

    def device(self, x=None, yh=None, c=None, yl=None, z=None):
        x = self.x if x is None else x
        yh = self.yh if yh is None else yh
        c = self.c if c is None else c
        yl = self.yl if yl is None else yl
        z = self.z if z is None else z
        return (yl * 8 + z, x * 4 + yh * 2 + c)

    def xs(self, dx):
        return lax.rem(self.x + (dx + 4), 4)


class Net:
    def __init__(self, send, recv, local):
        self.send, self.recv, self.local = send, recv, local
        self.n = 0
        self.m = 0
        self.all = []

    def go(self, src, dst, device):
        cp = pltpu.make_async_remote_copy(
            src_ref=src, dst_ref=dst, send_sem=self.send.at[self.n], recv_sem=self.recv.at[self.n],
            device_id=device, device_id_type=MESH,
        )
        self.n += 1
        cp.start()
        self.all.append(cp)
        return cp

    def make(self, src, dst, device):
        self.n += 1
        return pltpu.make_async_remote_copy(
            src_ref=src, dst_ref=dst, send_sem=self.send.at[self.n - 1], recv_sem=self.recv.at[self.n - 1],
            device_id=device, device_id_type=MESH,
        )

    def here(self, src, dst):
        cp = pltpu.make_async_copy(src, dst, self.local.at[self.m])
        self.m += 1
        cp.start()
        return cp

    def drain(self):
        for cp in self.all:
            cp.wait_send()


def greet(devices):
    barrier = pltpu.get_barrier_semaphore()
    for device in devices:
        pl.semaphore_signal(barrier, inc=1, device_id=device, device_id_type=MESH)
    pl.semaphore_wait(barrier, len(devices))


def rows_of(start, size, unit):
    return pl.ds(pl.multiple_of(start, unit), size)


NT = (((1,), (1,)), ((), ()))
TN = (((0,), (0,)), ((), ()))
N = 2 * ROWS
GC = 3 * GW
KW = 2 * GW


def step_kernel(x_ref, w_ref, g_ref, att, gi, gw,
                x2, w2, qg, kv, m_ref, l_ref, o_ref, stat_out, stat_in, lse_ref, delta_ref,
                o_out, o_in, o2, dq_ref, dq_out, dq_in, kpart, kother, ksib, kland, dproj,
                part, other, sibl, land_a, land_b, land_l, land_r,
                dfar, w3, zbuf, z_in, own, fin, send, recv, local):
    p = Place()
    net = Net(send, recv, local)
    ypair = p.device(yh=1 - p.yh)
    mirror = p.device(yh=1 - p.yh, yl=1 - p.yl)
    near = p.device(yl=1 - p.yl)
    right, left, sib = p.device(x=p.xs(1)), p.device(x=p.xs(-1)), p.device(c=1 - p.c)
    odd = lax.rem(p.x, 2)
    qpair, kpair = p.device(x=p.xs(1 - 2 * odd)), p.device(x=p.xs(2 * odd - 1))
    zs = [lax.rem(p.z + d, 8) for d in range(8)]
    greet([right, left, sib] + [
        p.device(yh=p.yh if a == 0 else 1 - p.yh, yl=p.yl if b == 0 else 1 - p.yl, z=zs[d])
        for d in range(8) for a in range(2) for b in range(2) if d + a + b > 0])

    def wrows(x, yh):
        return w2.at[rows_of((x * 4 + yh * 2 + p.c) * WROWS, WROWS, 32)]

    def wcols(yh, j):
        return w_ref.at[:, rows_of(yh * GW + 2 * GW * j, GW, 128)]

    mine = wrows(p.x, p.yh)
    theirs = [net.go(wcols(1 - p.yh, j), mine.at[:, pl.ds(j * GW, GW)], mirror) for j in range(3)]
    own_w = [net.here(wcols(p.yh, j), mine.at[:, pl.ds(j * GW, GW)]) for j in range(3)]
    my_rows = rows_of(p.yh * ROWS, ROWS, 64)
    far_rows = rows_of((1 - p.yh) * ROWS, ROWS, 64)
    for cp in own_w:
        cp.wait()
    a_right, a_left = net.go(mine, mine, right), net.go(mine, mine, left)
    relays = [net.go(mine, mine, sib)]

    def relay(x, yh):
        block = wrows(x, yh)
        relays.append(net.go(block, block, sib))

    qg[my_rows, pl.ds(GW, GW)] = g_ref[:, rows_of(p.yh * GW, GW, 128)]
    for cp in theirs:
        cp.wait_recv()
    xo = net.go(x_ref, x2.at[my_rows], ypair)
    block = wrows(p.x, 1 - p.yh)
    b_right, b_left = net.go(block, block, right), net.go(block, block, left)
    relay(p.x, 1 - p.yh)
    a_right.wait_recv()
    block = wrows(p.xs(-1), p.yh)
    f_right = net.go(block, block, right)
    relay(p.xs(-1), p.yh)
    a_left.wait_recv()
    relay(p.xs(1), p.yh)
    b_left.wait_recv()
    block = wrows(p.xs(1), 1 - p.yh)
    f_left = net.go(block, block, left)
    relay(p.xs(1), 1 - p.yh)
    b_right.wait_recv()
    relay(p.xs(-1), 1 - p.yh)
    go = net.go(g_ref.at[:, rows_of((1 - p.yh) * GW, GW, 128)], qg.at[my_rows, pl.ds(GW, GW)], ypair)
    f_right.wait_recv()
    relay(p.xs(2), p.yh)
    f_left.wait_recv()
    relay(p.xs(2), 1 - p.yh)
    for cp in relays:
        cp.wait_recv()

    half_w = rows_of(p.c * (D // 2), D // 2, 256)

    def project(tokens, rows, j):
        t = jnp.dot(tokens[...], w2[:, pl.ds(j * GW, GW)], preferred_element_type=F32).astype(BF)
        if j == 0:
            qg[rows, pl.ds(0, GW)] = t
        else:
            kv[0, p.c, rows, pl.ds((j - 1) * GW, GW)] = t

    def give(rows):
        mk, mq = kv.at[0, p.c, rows], qg.at[rows, pl.ds(0, GW)]
        out = [net.go(mk, kv.at[1, p.c, rows], kpair), net.go(mk, mk, sib)]
        return out, mq

    project(x_ref, my_rows, 1)
    project(x_ref, my_rows, 2)
    (k_a, s_a), mq = give(my_rows)
    project(x_ref, my_rows, 0)
    there = rows_of(N + p.yh * ROWS, ROWS, 64)
    q_a = net.go(mq, qg.at[there, pl.ds(0, GW)], qpair)
    xo.wait_recv()
    far_x = x2.at[far_rows]
    project(far_x, far_rows, 1)
    project(far_x, far_rows, 2)
    (k_b, s_b), mq = give(far_rows)
    project(far_x, far_rows, 0)
    there_b = rows_of(N + (1 - p.yh) * ROWS, ROWS, 64)
    q_b = net.go(mq, qg.at[there_b, pl.ds(0, GW)], qpair)
    g_cols = pl.ds(GW, GW)
    g_a = net.go(qg.at[my_rows, g_cols], qg.at[there, g_cols], qpair)
    go.wait_recv()
    g_b = net.go(qg.at[far_rows, g_cols], qg.at[there_b, g_cols], qpair)
    w_far = net.go(w2.at[half_w], w3.at[half_w], mirror)
    x2[my_rows, :] = x_ref[...]

    m_ref[...] = jnp.full_like(m_ref, -1e30)
    l_ref[...] = jnp.zeros_like(l_ref)
    o_ref[...] = jnp.zeros_like(o_ref)
    c2 = HALF_SCALE * LOG2E

    def forward(b, rows, lo, size):
        qr = pl.ds(lo, size)
        for h in range(GROUP):
            q = qg[qr, pl.ds(h * HEAD, HEAD)]
            keys = kv[b, :, rows, pl.ds(h * HEAD, HEAD)].reshape(N, HEAD)
            values = kv[b, :, rows, pl.ds(GW + h * HEAD, HEAD)].reshape(N, HEAD)
            s = lax.dot_general(keys, q, NT, preferred_element_type=F32) * c2
            hs, hr = pl.ds(h, 1), pl.ds(h * HEAD, HEAD)
            m_old = m_ref[hs, qr]
            m_new = jnp.maximum(m_old, jnp.max(s, axis=0, keepdims=True))
            alpha = jnp.exp2(m_old - m_new)
            e = jnp.exp2(s - m_new)
            m_ref[hs, qr] = m_new
            l_ref[hs, qr] = l_ref[hs, qr] * alpha + jnp.sum(e, axis=0, keepdims=True)
            o_ref[hr, qr] = o_ref[hr, qr] * alpha + jnp.dot(
                values.T, e.astype(BF), preferred_element_type=F32)

    s_a.wait_recv()
    forward(0, my_rows, 0, N)
    s_b.wait_recv()
    forward(0, far_rows, 0, N)
    k_a.wait_recv()
    t_a = net.go(kv.at[1, p.c, my_rows], kv.at[1, p.c, my_rows], sib)
    t_a.wait_recv()
    forward(1, my_rows, 0, N)
    q_a.wait_recv()
    q_b.wait_recv()
    forward(0, my_rows, N, N)
    forward(0, far_rows, N, N)
    forward(1, my_rows, N, N)
    k_b.wait_recv()
    t_b = net.go(kv.at[1, p.c, far_rows], kv.at[1, p.c, far_rows], sib)
    g_a.wait_recv()
    g_b.wait_recv()
    t_b.wait_recv()
    forward(1, far_rows, 0, 2 * N)

    stat_out[...] = jnp.zeros_like(stat_out)
    for h in range(GROUP):
        hr = pl.ds(h * HEAD, HEAD)
        stat_out[pl.ds(h, 1), :] = m_ref[pl.ds(h, 1), :]
        stat_out[pl.ds(GROUP + h, 1), :] = l_ref[pl.ds(h, 1), :]
        stat_out[pl.ds(2 * GROUP + h, 1), :] = jnp.sum(
            o_ref[hr, :] * qg[:, pl.ds(GW + h * HEAD, HEAD)].T.astype(F32), axis=0, keepdims=True)
    st = net.go(stat_out, stat_in, qpair)
    st.wait_recv()

    def stat(i):
        other_half = stat_in[pl.ds(i, 1), :]
        return stat_out[pl.ds(i, 1), :], jnp.concatenate([other_half[:, N:], other_half[:, :N]], axis=1)

    for h in range(GROUP):
        hs = pl.ds(h, 1)
        m1, m2 = stat(h)
        l1, l2 = stat(GROUP + h)
        d1, d2 = stat(2 * GROUP + h)
        m = jnp.maximum(m1, m2)
        f1, f2 = jnp.exp2(m1 - m), jnp.exp2(m2 - m)
        l = l1 * f1 + l2 * f2
        lse_ref[hs, :] = m + jnp.log2(l)
        delta_ref[hs, :] = (d1 * f1 + d2 * f2) / l
        l_ref[hs, :] = f1 / l
    dq_ref[...] = jnp.zeros_like(dq_ref)

    def backward(i, b, h, own_core):
        hr = pl.ds(h * HEAD, HEAD)
        c = p.c if own_core else 1 - p.c
        q, g = qg[:, hr], qg[:, pl.ds(GW + h * HEAD, HEAD)]
        k = kv[b, c, :, hr]
        s = lax.dot_general(k, q, NT, preferred_element_type=F32) * c2
        e = jnp.exp2(s - lse_ref[pl.ds(h, 1), :])
        dv = jnp.dot(e.astype(BF), g, preferred_element_type=F32).astype(BF)
        de = lax.dot_general(kv[b, c, :, pl.ds(GW + h * HEAD, HEAD)], g, NT, preferred_element_type=F32)
        ds = (e * (de - delta_ref[pl.ds(h, 1), :])).astype(BF)
        dk = (jnp.dot(ds, q, preferred_element_type=F32) * HALF_SCALE).astype(BF)
        dq_ref[hr, :] += jnp.dot(k.T, ds, preferred_element_type=F32)
        kpart[i, h, own_core, :, pl.ds(0, HEAD)] = dk
        kpart[i, h, own_core, :, pl.ds(HEAD, HEAD)] = dv
        return None if own_core else net.go(kpart.at[i, h, 0], ksib.at[i, h], sib)

    for h in range(GROUP):
        hr = pl.ds(h * HEAD, HEAD)
        o_ref[hr, :] = o_ref[hr, :] * l_ref[pl.ds(h, 1), :]
        o_out[hr, :] = o_ref[hr, pl.ds(N, N)].astype(BF)
    oc = net.go(o_out, o_in, qpair)
    lands = []
    for h in range(GROUP):
        cp = backward(0, 1, h, 0)
        backward(0, 1, h, 1)
        cp.wait_recv()
        kother[h] = (kpart[0, h, 1].astype(F32) + ksib[0, h].astype(F32)).astype(BF)
        lands.append(net.go(kother.at[h], kland.at[h], kpair))
    own_k, dqs = [], []
    for h in range(GROUP):
        hr = pl.ds(h * HEAD, HEAD)
        own_k.append(backward(1, 0, h, 0))
        backward(1, 0, h, 1)
        dq_out[hr, :] = (dq_ref[hr, pl.ds(N, N)] * HALF_SCALE).astype(BF)
        dqs.append(net.go(dq_out.at[hr], dq_in.at[hr], qpair))
    oc.wait_recv()
    for h in range(GROUP):
        hr = pl.ds(h * HEAD, HEAD)
        o2[:, hr] = (o_ref[hr, pl.ds(0, N)] + o_in[hr, :].astype(F32)).astype(BF).T
    cols = rows_of(p.yh * GW, GW, 128)
    ao = net.go(o2.at[far_rows], att.at[:, cols], ypair)
    al = net.here(o2.at[my_rows], att.at[:, cols])
    for h in range(GROUP):
        hr = pl.ds(h * HEAD, HEAD)
        dqs[h].wait_recv()
        dproj[:, hr] = (dq_ref[hr, pl.ds(0, N)] * HALF_SCALE + dq_in[hr, :].astype(F32)).astype(BF).T

    order = [p.xs(2), p.xs(1), p.xs(-1), p.x]
    jobs = [{} for _ in range(3)]

    def terms(j):
        jobs[j]["sib"] = []
        for i, x in enumerate(order):
            t = lax.dot_general(x2[:, rows_of(x * GW, GW, 128)], dproj[:, pl.ds(j * GW, GW)], TN,
                                preferred_element_type=F32).astype(BF)
            for c in range(2):
                for yh in range(2):
                    lo = (yh * 2 + c) * WROWS
                    part[j, i, c, yh] = t[lo:lo + WROWS]
            jobs[j]["sib"].append(net.go(part.at[j, i, 1 - p.c], sibl.at[j, i], sib))

    def add(j, i, yh, *lands):
        t = part[j, i, p.c, yh].astype(F32) + sibl[j, i, yh].astype(F32)
        for ref in lands:
            t = t + ref.astype(F32)
        return t

    def x_first(j):
        jobs[j]["sib"][0].wait_recv()
        for yh in range(2):
            other[j, 0, yh] = add(j, 0, yh).astype(BF)
        jobs[j]["a"] = net.go(other.at[j, 0, 0], land_a.at[j], right)
        jobs[j]["b"] = net.go(other.at[j, 0, 1], land_b.at[j], left)

    def x_second(j):
        job = jobs[j]
        job["sib"][1].wait_recv()
        job["sib"][2].wait_recv()
        other[j, 1, 1] = add(j, 1, 1).astype(BF)
        other[j, 2, 0] = add(j, 2, 0).astype(BF)
        job["a"].wait_recv()
        other[j, 1, 0] = add(j, 1, 0, land_a[j]).astype(BF)
        job["l"] = net.go(other.at[j, 1], land_l.at[j], right)
        job["b"].wait_recv()
        other[j, 2, 1] = add(j, 2, 1, land_b[j]).astype(BF)
        job["r"] = net.go(other.at[j, 2], land_r.at[j], left)

    def peer(yl, d, yh=None):
        return p.device(yh=yh, yl=yl, z=zs[d])

    def piece(z):
        return rows_of(z * 48, 48, 16)

    def dp_sum(j):
        job = jobs[j]
        job["sib"][3].wait_recv()
        job["l"].wait_recv()
        job["r"].wait_recv()
        for r in range(2):
            t = add(j, 3, r, land_l[j, r], land_r[j, r]).astype(BF)
            for i in range(3):
                zbuf[j, r, pl.ds(i * WROWS, WROWS), :] = t[:, i * 128:(i + 1) * 128]
        job["z"] = []
        for d in (4, 3, 5, 2, 6, 1, 7, 0):
            for a in ((0, 1) if d else (1,)):
                yl = p.yl if a == 0 else 1 - p.yl
                target = zs[d]
                cp = net.make(zbuf.at[j, lax.rem(p.yh + yl, 2), piece(lax.rem(target, 6))],
                              z_in.at[j, a * 8 + d], peer(yl, d))
                job["z"].append((cp, target, a * 8 + d))

                @pl.when(target < 6)
                def _(cp=cp):
                    cp.start()

    def dp_share(j):
        job = jobs[j]

        @pl.when(p.z < 6)
        def _():
            r = lax.rem(p.yh + p.yl, 2)
            t = zbuf[j, r, piece(p.z), :].astype(F32)
            for cp, _, slot in job["z"]:
                cp.wait_recv()
                t = t + z_in[j, slot].astype(F32)
            own[j] = t.astype(BF)

            @pl.when(p.yl == 0)
            def _():
                fin[j, 0, piece(p.z), :] = own[j]

        for cp, target, _ in job["z"]:
            @pl.when(target < 6)
            def _(cp=cp):
                cp.wait_send()

        job["f"] = []
        base = net.n
        net.n += 16
        for d in (4, 3, 5, 2, 6, 1, 7, 0):
            for yl in range(2):
                cp = pltpu.make_async_remote_copy(
                    src_ref=own.at[j], dst_ref=fin.at[j, p.yl, piece(lax.rem(p.z, 6))],
                    send_sem=send.at[base + yl * 8 + d], recv_sem=recv.at[base + p.yl * 8 + d],
                    device_id=peer(yl, d, lax.rem(p.yh + p.yl, 2)), device_id_type=MESH)
                source = lax.rem(p.z + (8 - d), 8)
                land = fin.at[j, yl, piece(lax.rem(source, 6))]
                arrive = pltpu.make_async_remote_copy(
                    src_ref=land, dst_ref=land, send_sem=send.at[base + yl * 8 + d],
                    recv_sem=recv.at[base + yl * 8 + d], device_id=right, device_id_type=MESH)
                real = p.z < 6
                comes = source < 6
                if d == 0 and yl == 0:
                    real = jnp.logical_and(real, p.yl == 1)
                    comes = jnp.logical_and(comes, p.yl == 1)
                job["f"].append((cp, real, arrive, comes))

                @pl.when(real)
                def _(cp=cp):
                    cp.start()

    def write(j):
        for cp, real, arrive, comes in jobs[j]["f"]:
            @pl.when(comes)
            def _(arrive=arrive):
                arrive.wait_recv()

            @pl.when(real)
            def _(cp=cp):
                cp.wait_send()

        for g in range(2):
            t = fin[j, lax.rem(p.yh + g, 2)]
            for i in range(3):
                gw[:, pl.ds(j * 2 * GW + g * GW + i * 128, 128)] = t[i * WROWS:(i + 1) * WROWS]

    def far(j):
        part_cols = pl.ds(j * GW, GW)
        return net.go(dproj.at[far_rows, part_cols], dfar.at[:, part_cols], ypair)

    fars = [far(0)]
    terms(0)
    x_first(0)
    for h in range(GROUP):
        own_k[h].wait_recv()
        lands[h].wait_recv()
        t = kpart[1, h, 1].astype(F32) + ksib[1, h].astype(F32) + kland[h].astype(F32)
        dproj[:, pl.ds(GW + h * HEAD, HEAD)] = t[:, :HEAD].astype(BF)
        dproj[:, pl.ds(2 * GW + h * HEAD, HEAD)] = t[:, HEAD:].astype(BF)
    fars += [far(1), far(2)]
    terms(1)
    terms(2)
    x_second(0)
    x_first(1)
    x_first(2)
    dp_sum(0)
    x_second(1)
    x_second(2)
    w_far.wait_recv()
    w_sib = net.go(w3.at[half_w], w3.at[half_w], sib)
    dp_share(0)
    dp_sum(1)
    part_gi = lax.dot_general(dproj[my_rows, :], w2[...], NT, preferred_element_type=F32)
    dp_sum(2)
    dp_share(1)
    w_sib.wait_recv()
    for cp in fars:
        cp.wait_recv()
    gi[...] = (part_gi + lax.dot_general(dfar[...], w3[...], NT, preferred_element_type=F32)).astype(BF)
    dp_share(2)
    write(0)
    write(1)
    write(2)
    al.wait()
    ao.wait_recv()
    net.drain()


VMEM = pl.BlockSpec(memory_space=pltpu.VMEM)


def on_device(seq_embed, w_qkv, upstream):
    scratch = [
        ((N, D), BF), ((D, GC), BF), ((2 * N, KW), BF), ((2, 2, N, KW), BF),
        ((8, 2 * N), F32), ((8, 2 * N), F32), ((GW, 2 * N), F32), ((16, 2 * N), F32), ((16, 2 * N), F32),
        ((8, 2 * N), F32), ((8, 2 * N), F32),
        ((GW, N), BF), ((GW, N), BF), ((N, GW), BF), ((GW, 2 * N), F32), ((GW, N), BF), ((GW, N), BF),
        ((2, GROUP, 2, N, 2 * HEAD), BF), ((GROUP, N, 2 * HEAD), BF), ((2, GROUP, N, 2 * HEAD), BF),
        ((GROUP, N, 2 * HEAD), BF), ((N, GC), BF),
        ((3, 4, 2, 2, WROWS, GW), BF), ((3, 3, 2, WROWS, GW), BF), ((3, 4, 2, WROWS, GW), BF),
        ((3, WROWS, GW), BF), ((3, WROWS, GW), BF), ((3, 2, WROWS, GW), BF), ((3, 2, WROWS, GW), BF),
        ((ROWS, GC), BF), ((D, GC), BF),
        ((3, 2, 288, 128), BF), ((3, 16, 48, 128), BF), ((3, 48, 128), BF), ((3, 2, 288, 128), BF),
    ]
    copies = 192
    att, gi, gw = pl.pallas_call(
        step_kernel,
        out_shape=[jax.ShapeDtypeStruct(s, BF) for s in ((ROWS, KW), (ROWS, D), (WROWS, 2 * GC))],
        in_specs=[VMEM] * 3,
        out_specs=[VMEM] * 3,
        scratch_shapes=[pltpu.VMEM(s, t) for s, t in scratch] + [
            pltpu.SemaphoreType.DMA((copies,)), pltpu.SemaphoreType.DMA((copies,)),
            pltpu.SemaphoreType.DMA((8,))],
        compiler_params=pltpu.CompilerParams(
            collective_id=0, has_side_effects=True, vmem_limit_bytes=58 * 2**20),
    )(seq_embed[0], w_qkv, upstream[0])
    return att[None], gi[None], gw


def solution(mesh):
    placed = (P("dp", "seq", None), P("seq", None), P("dp", "seq", None))
    return jax.shard_map(
        on_device,
        mesh=mesh,
        in_specs=placed,
        out_specs=(P("dp", "seq", None), P("dp", "seq", None), P("seq", None)),
        check_vma=False,
    )
```

time: 131 us -> 119 us (0.908); the launches traced: 131 us -> 118 us
  Pallas kernels: 127 us -> 113 us
    pallas_call x1, Pallas kernels: 127 us -> 113 us  [on_device(): pl.pallas_call(step_kernel, out_shape=[jax.ShapeDtypeStruct(s, BF) for s...]
where the time goes in v3:
time: 119 us; the launch traced here: 118 us
  Pallas kernels  113 us (95%)
  local copies, waits for them, and re-layouts  3.75 us (3%)
    pallas_call x1, Pallas kernels, on_device(): pl.pallas_call(step_kernel, out_shape=[jax.ShapeDtypeStruct(s, BF) for s...  113 us
    unnamed x7, local copies, waits for them, and re-layouts  3.75 us

profile of v3, /device:TPU:2, one launch (start us, length us, event | category | flops | bytes accessed | tf_op | source)
XLA Modules:
  0.0 117.6 jit_solution(5042321676740951869)
XLA Ops:
  0.6 113.2 %shard_map.58 = (bf16[192,768]{1,0:T(8,128)(2,1)}, bf16[192,1536]{1,0:T(8,128)(2,1)}, bf16[96,2304]{1,0:T(8,128)(2,1)}) custom-call(bf16[192,1536]{1,0:T(8,128)(2,1)} %bitcast.5, bf16[96,2304]{1,0:T(8,128)(2,1)} %w_ref.1, bf16[192,768]{1,0:T(8,128)(2,1)} %bitcast.7), custom_call_target="tpu_custom_call" | custom-call | tf_op jit(solution)/shard_map/pallas_call | solution.py:498
  113.8 0.0 copy-start
  113.8 1.8 %copy.9 = bf16[1,192,768]{2,1,0:T(8,128)(2,1)} copy(bf16[1,192,768]{2,1,0:T(8,128)(2,1)} %bitcast.6) | data formatting | bytes 589824
  115.6 0.0 copy-done
  115.6 0.0 copy-start.1
  115.6 0.8 copy.10
  116.4 0.4 copy-done.1
  116.8 0.8 copy.11
Async XLA Ops:
  113.8 1.8 %copy-start = (bf16[192,1536]{1,0:T(8,128)(2,1)S(1)}, bf16[192,1536]{1,0:T(8,128)(2,1)}, u32[]{:S(2)}) copy-start(bf16[192,1536]{1,0:T(8,128)(2,1)} %get-tuple-element.7) | copy-start | bytes 1769476
  115.6 1.2 %copy-start.1 = (bf16[96,2304]{1,0:T(8,128)(2,1)S(1)}, bf16[96,2304]{1,0:T(8,128)(2,1)}, u32[]{:S(2)}) copy-start(bf16[96,2304]{1,0:T(8,128)(2,1)} %get-tuple-element.14) | copy-start | bytes 1327108

commit v4 on v3

--- a/solution.py
+++ b/solution.py
@@ -105,21 +105,23 @@
     odd = lax.rem(p.x, 2)
     qpair, kpair = p.device(x=p.xs(1 - 2 * odd)), p.device(x=p.xs(2 * odd - 1))
     zs = [lax.rem(p.z + d, 8) for d in range(8)]
+
+    def wrows(x, yh):
+        return w2.at[rows_of((x * 4 + yh * 2 + p.c) * WROWS, WROWS, 32)]
+
+    def wcols(yh, j):
+        return w_ref.at[:, rows_of(yh * GW + 2 * GW * j, GW, 128)]
+
+    mine = wrows(p.x, p.yh)
+    my_rows = rows_of(p.yh * ROWS, ROWS, 64)
+    far_rows = rows_of((1 - p.yh) * ROWS, ROWS, 64)
+    own_w = [net.here(wcols(p.yh, j), mine.at[:, pl.ds(j * GW, GW)]) for j in range(3)]
+    own_x = net.here(x_ref, x2.at[my_rows])
+    own_g = net.here(g_ref.at[:, rows_of(p.yh * GW, GW, 128)], qg.at[my_rows, pl.ds(GW, GW)])
     greet([right, left, sib] + [
         p.device(yh=p.yh if a == 0 else 1 - p.yh, yl=p.yl if b == 0 else 1 - p.yl, z=zs[d])
         for d in range(8) for a in range(2) for b in range(2) if d + a + b > 0])
-
-    def wrows(x, yh):
-        return w2.at[rows_of((x * 4 + yh * 2 + p.c) * WROWS, WROWS, 32)]
-
-    def wcols(yh, j):
-        return w_ref.at[:, rows_of(yh * GW + 2 * GW * j, GW, 128)]
-
-    mine = wrows(p.x, p.yh)
     theirs = [net.go(wcols(1 - p.yh, j), mine.at[:, pl.ds(j * GW, GW)], mirror) for j in range(3)]
-    own_w = [net.here(wcols(p.yh, j), mine.at[:, pl.ds(j * GW, GW)]) for j in range(3)]
-    my_rows = rows_of(p.yh * ROWS, ROWS, 64)
-    far_rows = rows_of((1 - p.yh) * ROWS, ROWS, 64)
     for cp in own_w:
         cp.wait()
     a_right, a_left = net.go(mine, mine, right), net.go(mine, mine, left)
@@ -129,10 +131,12 @@
         block = wrows(x, yh)
         relays.append(net.go(block, block, sib))
 
-    qg[my_rows, pl.ds(GW, GW)] = g_ref[:, rows_of(p.yh * GW, GW, 128)]
+    own_x.wait()
+    own_g.wait()
     for cp in theirs:
         cp.wait_recv()
-    xo = net.go(x_ref, x2.at[my_rows], ypair)
+    mine_x = x2.at[my_rows]
+    xo = net.go(mine_x, mine_x, ypair)
     block = wrows(p.x, 1 - p.yh)
     b_right, b_left = net.go(block, block, right), net.go(block, block, left)
     relay(p.x, 1 - p.yh)
@@ -170,10 +174,10 @@
         out = [net.go(mk, kv.at[1, p.c, rows], kpair), net.go(mk, mk, sib)]
         return out, mq
 
-    project(x_ref, my_rows, 1)
-    project(x_ref, my_rows, 2)
+    project(mine_x, my_rows, 1)
+    project(mine_x, my_rows, 2)
     (k_a, s_a), mq = give(my_rows)
-    project(x_ref, my_rows, 0)
+    project(mine_x, my_rows, 0)
     there = rows_of(N + p.yh * ROWS, ROWS, 64)
     q_a = net.go(mq, qg.at[there, pl.ds(0, GW)], qpair)
     xo.wait_recv()
@@ -189,19 +193,21 @@
     go.wait_recv()
     g_b = net.go(qg.at[far_rows, g_cols], qg.at[there_b, g_cols], qpair)
     w_far = net.go(w2.at[half_w], w3.at[half_w], mirror)
-    x2[my_rows, :] = x_ref[...]
 
     m_ref[...] = jnp.full_like(m_ref, -1e30)
     l_ref[...] = jnp.zeros_like(l_ref)
     o_ref[...] = jnp.zeros_like(o_ref)
     c2 = HALF_SCALE * LOG2E
 
-    def forward(b, rows, lo, size):
+    def forward(b, rows, lo, size, core=None):
         qr = pl.ds(lo, size)
         for h in range(GROUP):
             q = qg[qr, pl.ds(h * HEAD, HEAD)]
-            keys = kv[b, :, rows, pl.ds(h * HEAD, HEAD)].reshape(N, HEAD)
-            values = kv[b, :, rows, pl.ds(GW + h * HEAD, HEAD)].reshape(N, HEAD)
+            k_cols, v_cols = pl.ds(h * HEAD, HEAD), pl.ds(GW + h * HEAD, HEAD)
+            if core is None:
+                keys, values = kv[b, :, rows, k_cols].reshape(N, HEAD), kv[b, :, rows, v_cols].reshape(N, HEAD)
+            else:
+                keys, values = kv[b, core, rows, k_cols], kv[b, core, rows, v_cols]
             s = lax.dot_general(keys, q, NT, preferred_element_type=F32) * c2
             hs, hr = pl.ds(h, 1), pl.ds(h * HEAD, HEAD)
             m_old = m_ref[hs, qr]
@@ -228,10 +234,11 @@
     forward(1, my_rows, N, N)
     k_b.wait_recv()
     t_b = net.go(kv.at[1, p.c, far_rows], kv.at[1, p.c, far_rows], sib)
+    forward(1, far_rows, 0, 2 * N, p.c)
+    t_b.wait_recv()
+    forward(1, far_rows, 0, 2 * N, 1 - p.c)
     g_a.wait_recv()
     g_b.wait_recv()
-    t_b.wait_recv()
-    forward(1, far_rows, 0, 2 * N)
 
     stat_out[...] = jnp.zeros_like(stat_out)
     for h in range(GROUP):
@@ -308,11 +315,11 @@
         dproj[:, hr] = (dq_ref[hr, pl.ds(0, N)] * HALF_SCALE + dq_in[hr, :].astype(F32)).astype(BF).T
 
     order = [p.xs(2), p.xs(1), p.xs(-1), p.x]
-    jobs = [{} for _ in range(3)]
-
-    def terms(j):
-        jobs[j]["sib"] = []
-        for i, x in enumerate(order):
+    jobs = [{"sib": []} for _ in range(3)]
+
+    def terms(j, blocks):
+        for i in blocks:
+            x = order[i]
             t = lax.dot_general(x2[:, rows_of(x * GW, GW, 128)], dproj[:, pl.ds(j * GW, GW)], TN,
                                 preferred_element_type=F32).astype(BF)
             for c in range(2):
@@ -441,7 +448,8 @@
         return net.go(dproj.at[far_rows, part_cols], dfar.at[:, part_cols], ypair)
 
     fars = [far(0)]
-    terms(0)
+    terms(0, (0,))
+    terms(0, (1, 2, 3))
     x_first(0)
     for h in range(GROUP):
         own_k[h].wait_recv()
@@ -450,14 +458,18 @@
         dproj[:, pl.ds(GW + h * HEAD, HEAD)] = t[:, :HEAD].astype(BF)
         dproj[:, pl.ds(2 * GW + h * HEAD, HEAD)] = t[:, HEAD:].astype(BF)
     fars += [far(1), far(2)]
-    terms(1)
-    terms(2)
+    terms(1, (0,))
+    terms(2, (0,))
     x_second(0)
     x_first(1)
     x_first(2)
+    terms(1, (1, 2))
+    terms(2, (1, 2))
     dp_sum(0)
     x_second(1)
     x_second(2)
+    terms(1, (3,))
+    terms(2, (3,))
     w_far.wait_recv()
     w_sib = net.go(w3.at[half_w], w3.at[half_w], sib)
     dp_share(0)
@@ -465,11 +477,11 @@
     part_gi = lax.dot_general(dproj[my_rows, :], w2[...], NT, preferred_element_type=F32)
     dp_sum(2)
     dp_share(1)
+    dp_share(2)
     w_sib.wait_recv()
     for cp in fars:
         cp.wait_recv()
     gi[...] = (part_gi + lax.dot_general(dfar[...], w3[...], NT, preferred_element_type=F32)).astype(BF)
-    dp_share(2)
     write(0)
     write(1)
     write(2)
@@ -478,7 +490,21 @@
     net.drain()
 
 
+def copy_kernel(att, gi, gw, att_out, gi_out, gw_out, a, b, c, sems):
+    jobs = ((att, a, att_out.at[0]), (gi, b, gi_out.at[0]), (gw, c, gw_out))
+    into = [pltpu.make_async_copy(src, mid, sems.at[i]) for i, (src, mid, _) in enumerate(jobs)]
+    back = [pltpu.make_async_copy(mid, dst, sems.at[3 + i]) for i, (_, mid, dst) in enumerate(jobs)]
+    for cp in into:
+        cp.start()
+    for x, y in zip(into, back):
+        x.wait()
+        y.start()
+    for cp in back:
+        cp.wait()
+
+
 VMEM = pl.BlockSpec(memory_space=pltpu.VMEM)
+ANY = pl.BlockSpec(memory_space=pl.ANY)
 
 
 def on_device(seq_embed, w_qkv, upstream):
@@ -498,7 +524,7 @@
     att, gi, gw = pl.pallas_call(
         step_kernel,
         out_shape=[jax.ShapeDtypeStruct(s, BF) for s in ((ROWS, KW), (ROWS, D), (WROWS, 2 * GC))],
-        in_specs=[VMEM] * 3,
+        in_specs=[ANY] * 3,
         out_specs=[VMEM] * 3,
         scratch_shapes=[pltpu.VMEM(s, t) for s, t in scratch] + [
             pltpu.SemaphoreType.DMA((copies,)), pltpu.SemaphoreType.DMA((copies,)),
@@ -506,7 +532,14 @@
         compiler_params=pltpu.CompilerParams(
             collective_id=0, has_side_effects=True, vmem_limit_bytes=58 * 2**20),
     )(seq_embed[0], w_qkv, upstream[0])
-    return att[None], gi[None], gw
+    return pl.pallas_call(
+        copy_kernel,
+        out_shape=[jax.ShapeDtypeStruct(s, BF) for s in ((1, ROWS, KW), (1, ROWS, D), (WROWS, 2 * GC))],
+        in_specs=[ANY] * 3,
+        out_specs=[ANY] * 3,
+        scratch_shapes=[pltpu.VMEM(s, BF) for s in ((ROWS, KW), (ROWS, D), (WROWS, 2 * GC))] + [
+            pltpu.SemaphoreType.DMA((6,))],
+    )(att, gi, gw)
 
 
 def solution(mesh):

time: 119 us -> 116 us (0.975)
  local copies, waits for them, and re-layouts: 3.75 us -> 0 us
    unnamed x7 -> x0, local copies, waits for them, and re-layouts: 3.75 us -> none
    pallas_call x0 -> x1, Pallas kernels: none -> 2.16 us  [on_device(): pl.pallas_call(copy_kernel, out_shape=[jax.ShapeDtypeStruct(s, BF) for s...]
where the time goes in v4:
time: 116 us; the launch traced here: 115 us
  Pallas kernels  114 us (98%)
    pallas_call x1, Pallas kernels, on_device(): pl.pallas_call(step_kernel, out_shape=[jax.ShapeDtypeStruct(s, BF) for s...  112 us

profile of v4, /device:TPU:2, one launch (start us, length us, event | category | flops | bytes accessed | tf_op | source)
XLA Modules:
  0.0 115.1 jit_solution(12525615956314316833)
XLA Ops:
  0.6 112.1 %shard_map.58 = (bf16[192,768]{1,0:T(8,128)(2,1)}, bf16[192,1536]{1,0:T(8,128)(2,1)}, bf16[96,2304]{1,0:T(8,128)(2,1)}) custom-call(bf16[192,1536]{1,0:T(8,128)(2,1)} %bitcast.2, bf16[96,2304]{1,0:T(8,128)(2,1)} %w_ref.1, bf16[192,768]{1,0:T(8,128)(2,1)} %bitcast.3), custom_call_target="tpu_custom_call" | custom-call | tf_op jit(solution)/shard_map/pallas_call | solution.py:524
  112.7 2.2 %shard_map.59 = (bf16[1,192,768]{2,1,0:T(8,128)(2,1)}, bf16[1,192,1536]{2,1,0:T(8,128)(2,1)}, bf16[96,2304]{1,0:T(8,128)(2,1)}) custom-call(bf16[192,768]{1,0:T(8,128)(2,1)} %get-tuple-element.6.att, bf16[192,1536]{1,0:T(8,128)(2,1)} %get-tuple-element.7.gi, bf16[96,2304]{1,0:T(8,128)(2,1)} %get-tuple-element.8.gw), custom_call_target="tpu_custom_call" | custom-call | tf_op jit(solution)/shard_map/pallas_call | solution.py:535

commit v5 on v4

--- a/solution.py
+++ b/solution.py
@@ -474,10 +474,10 @@
     w_sib = net.go(w3.at[half_w], w3.at[half_w], sib)
     dp_share(0)
     dp_sum(1)
-    part_gi = lax.dot_general(dproj[my_rows, :], w2[...], NT, preferred_element_type=F32)
     dp_sum(2)
     dp_share(1)
     dp_share(2)
+    part_gi = lax.dot_general(dproj[my_rows, :], w2[...], NT, preferred_element_type=F32)
     w_sib.wait_recv()
     for cp in fars:
         cp.wait_recv()

time: 116 us -> 116 us (level)
  no operation moved by 1% of the time
where the time goes in v5:
time: 116 us; the launch traced here: 115 us
  Pallas kernels  114 us (98%)
    pallas_call x1, Pallas kernels, on_device(): pl.pallas_call(step_kernel, out_shape=[jax.ShapeDtypeStruct(s, BF) for s...  112 us

profile of v5, /device:TPU:2, one launch (start us, length us, event | category | flops | bytes accessed | tf_op | source)
XLA Modules:
  0.0 115.1 jit_solution(2243842922033503681)
XLA Ops:
  0.6 112.1 %shard_map.58 = (bf16[192,768]{1,0:T(8,128)(2,1)}, bf16[192,1536]{1,0:T(8,128)(2,1)}, bf16[96,2304]{1,0:T(8,128)(2,1)}) custom-call(bf16[192,1536]{1,0:T(8,128)(2,1)} %bitcast.2, bf16[96,2304]{1,0:T(8,128)(2,1)} %w_ref.1, bf16[192,768]{1,0:T(8,128)(2,1)} %bitcast.3), custom_call_target="tpu_custom_call" | custom-call | tf_op jit(solution)/shard_map/pallas_call | solution.py:524
  112.7 2.2 %shard_map.59 = (bf16[1,192,768]{2,1,0:T(8,128)(2,1)}, bf16[1,192,1536]{2,1,0:T(8,128)(2,1)}, bf16[96,2304]{1,0:T(8,128)(2,1)}) custom-call(bf16[192,768]{1,0:T(8,128)(2,1)} %get-tuple-element.6.att, bf16[192,1536]{1,0:T(8,128)(2,1)} %get-tuple-element.7.gi, bf16[96,2304]{1,0:T(8,128)(2,1)} %get-tuple-element.8.gw), custom_call_target="tpu_custom_call" | custom-call | tf_op jit(solution)/shard_map/pallas_call | solution.py:535
